TPU v7x, 256 devices: a whole 4x4x8 slice. The times are simulated.
256 devices in a mesh: form: 64 (over z, x, core), focus: 4 (over y).
Axes of the slice: x: 4, y: 4, z: 8, core: 2. Of those that a mesh axis runs over, the one named last changes fastest.
Arguments:
- echoes: bfloat16 [2, 8192, 32768], P(None, ('form', 'focus')), may hold values from -6 to 6
- scale_rate: float32 [8192], P(('form', 'focus')), may hold values from 8 to 40
- migration: float32 [8192], P(('form', 'focus')), may hold values from -48 to 48
- range_phase: float32 [32768], replicated, may hold values from -3.140625 to 3.140625
- azimuth_rate: float32 [32768], P(('form', 'focus')), may hold values from 40 to 400
- bright_columns: int32 [64, 32], P('form'), may hold values from 0 to 511, as said below
- line_block: int32 [64, 32, 1], P('form'), may hold values from 0 to 255
- line_center: int32 [64, 32], P('form'), may hold values from 0 to 8191
Outputs:
- focused_image: bfloat16 [2, 8192, 32768], P(None, None, ('form', 'focus'))
- phase_map: float32 [256, 256], P(('form', 'focus'))
Inputs may be any that keep to these rules, and one draw needn't show every extreme that they name: bright_columns[j, i] counts among the 512 range columns of form group j; columns may repeat. `line_block`: every map row is fed by at least one line.
All inputs are finite; a program needn't handle non-finite values.
Results may differ from a plain program's by a relative error of at most 0.02.
Values may be sent and summed in bfloat16 or wider, within the bound.
A program may use at most 128 MiB of HBM per device.

v0:
```python
import functools
import math

import jax
import jax.numpy as jnp
import ml_dtypes
import numpy as np
from jax import lax
from jax.experimental import pallas as pl
from jax.experimental.pallas import tpu as pltpu
from jax.sharding import PartitionSpec as P

R1 = 256
R2 = 128
NBLK = 256
AZ = 8192
CHUNKS = 4
LINES = 8
MESH = pl.DeviceIdType.MESH
F32 = jnp.float32
BF16 = jnp.bfloat16

TWO_PI = 2.0 * math.pi
EPSILON = 1e-06


def real_blocks(values):
    upper = np.stack([values.real, -values.imag], axis=-2)
    lower = np.stack([values.imag, values.real], axis=-2)
    return np.stack([upper, lower], axis=-4)


def unit(turns):
    return np.exp(2j * np.pi * turns)


def range_tables():
    k = np.arange(R1)
    n = np.arange(R2)
    wide = np.outer(k, k) % R1 / R1
    narrow = np.outer(n, n) % R2 / R2
    first = real_blocks(unit(-wide) / 16).reshape(2 * R1, 2 * R1)
    last = real_blocks(unit(wide) / 16).reshape(2 * R1, 2 * R1)
    inner = real_blocks(unit(-narrow) / math.sqrt(R2)).reshape(2 * R2, 2 * R2).T
    outer = real_blocks(unit(narrow) / math.sqrt(R2)).reshape(2 * R2, 2 * R2).T
    twist = unit(np.outer(k, n) / (R1 * R2))
    length = R1 * R2
    offsets = (k[:, None] * R2 + n[None, :] - length // 2) / length
    bins = k[:, None] + R1 * n[None, :]
    signed = np.where(bins >= length // 2, bins - length, bins) / length
    planes = np.stack([twist.real, twist.imag, offsets * offsets / TWO_PI, signed])
    swap = np.eye(256).reshape(LINES, 2, 16, 256).transpose(2, 1, 0, 3).reshape(256, 256)
    half = [t.astype(ml_dtypes.bfloat16) for t in (first, inner, outer, last, swap)]
    return half + [planes.astype(np.float32)]


def spread(blocks):
    full = np.einsum("...atcf,lm->...talfcm", blocks, np.eye(LINES))
    return full.reshape(*blocks.shape[:-4], 256, 256).astype(ml_dtypes.bfloat16)


def azimuth_tables():
    i = np.arange(16)
    near = np.outer(i, i) / 16
    shift = (i[:, None] * i[None, :] / 256)
    first = spread(real_blocks(unit(-near[None] - shift[:, :, None]) / 4))
    second = spread(real_blocks(unit(-near) / 4))
    third = spread(real_blocks(unit(near[None] + shift[:, :, None]) / 4))
    fourth = spread(real_blocks(unit(near) / 4))
    ks, l, m = np.arange(256)[:, None, None], np.arange(32), np.arange(32)
    turns = l[None, None, :] * ks / AZ + m[None, :, None] * l[None, None, :] / 32
    fwd = real_blocks(unit(-turns) / math.sqrt(32)).reshape(256, 2, 32, 2, 4, 8)
    fwd = fwd.transpose(0, 1, 2, 4, 3, 5).reshape(256, 64, 64)
    back = real_blocks(unit(turns.transpose(0, 2, 1)) / math.sqrt(32)).reshape(256, 2, 4, 8, 2, 32)
    back = back.transpose(0, 2, 1, 3, 4, 5).reshape(256, 64, 64)
    middle = np.concatenate([fwd, back], axis=2).astype(ml_dtypes.bfloat16)
    return first, second, middle, third, fourth


def cos_sin(turns):
    rest = turns - jnp.round(turns)
    z = rest * rest
    sine = rest * (6.28316395 + z * (-10.3342826 + z * (5.08377413 - 1.1092177 * z)))
    cosine = 0.99999995 + z * (-4.93479283 + z * (4.05841135 + z * (-1.33187657 + 0.21968961 * z)))
    return 1.0 - 0.5 * (sine * sine), sine * cosine


def dot(a, b):
    return jnp.dot(a, b, preferred_element_type=F32)


def range_kernel(
    x_hbm, rate, shift, rp, first, inner, outer, last, swap, planes, out_hbm,
    xbuf, rows, send, in_sem, send_sem, recv_sem, own_sem, *, talk=True,
):
    loads = [
        pltpu.make_async_copy(x_hbm.at[:, pl.ds(LINES * c, LINES)], xbuf.at[c], in_sem.at[c])
        for c in range(CHUNKS)
    ]
    for load in loads:
        load.start()
    if talk:
        form = lax.axis_index("form")
        focus = lax.axis_index("focus")
        me = form * 4 + focus

    def chunk(c, _):
        pltpu.make_async_copy(x_hbm.at[:, pl.ds(LINES * c, LINES)], xbuf.at[c], in_sem.at[c]).wait()

        def two_lines(p, _):
            parts = []
            for i in range(2):
                l = 2 * p + i
                cosine, sine = cos_sin(rate[LINES * c + l] * planes[2])
                re = xbuf[c, 0, l].astype(F32)
                im = xbuf[c, 1, l].astype(F32)
                parts.append(
                    jnp.concatenate(
                        [
                            (re * cosine - im * sine).astype(BF16),
                            (re * sine + im * cosine).astype(BF16),
                        ],
                        axis=0,
                    )
                )
            u = dot(first[...], jnp.concatenate(parts, axis=1))
            parts = []
            for i in range(2):
                lanes = slice(R2 * i, R2 * i + R2)
                re, im = u[:R1, lanes], u[R1:, lanes]
                cosine, sine = planes[0], planes[1]
                twisted = jnp.concatenate(
                    [
                        (re * cosine + im * sine).astype(BF16),
                        (im * cosine - re * sine).astype(BF16),
                    ],
                    axis=1,
                )
                spectrum = dot(twisted, inner[...])
                re, im = spectrum[:, :R2], spectrum[:, R2:]
                cosine, sine = cos_sin(rp[...] + shift[LINES * c + 2 * p + i] * planes[3])
                matched = jnp.concatenate(
                    [
                        (re * cosine + im * sine).astype(BF16),
                        (im * cosine - re * sine).astype(BF16),
                    ],
                    axis=1,
                )
                w = dot(matched, outer[...])
                re, im = w[:, :R2], w[:, R2:]
                cosine, sine = planes[0], planes[1]
                parts.append(
                    jnp.concatenate(
                        [
                            (re * cosine - im * sine).astype(BF16),
                            (re * sine + im * cosine).astype(BF16),
                        ],
                        axis=0,
                    )
                )
            done = dot(last[...], jnp.concatenate(parts, axis=1)).astype(BF16)
            for i in range(2):
                for a in range(2):
                    rows[2 * p + i, a] = done[R1 * a : R1 * a + R1, R2 * i : R2 * i + R2]
            return 0

        lax.fori_loop(0, LINES // 2, two_lines, 0)

        def swapped(t, _):
            cut = [
                rows[:, :, pl.ds(pl.multiple_of(32 * t + 16 * i, 16), 16)].reshape(256, R2)
                for i in range(2)
            ]
            out = dot(swap[...], jnp.concatenate(cut, axis=1)).astype(BF16)
            for i in range(2):
                send[c, pl.ds(32 * t + 16 * i, 16)] = out[:, R2 * i : R2 * i + R2].reshape(16, 16, R2)
            return 0

        lax.fori_loop(0, 8, swapped, 0, unroll=2)
        if not talk:
            return 0
        pltpu.make_async_copy(send.at[c, me], out_hbm.at[c, me], own_sem).start()

        def sends(j, _):
            dy = lax.rem(j, 4)
            other = focus + dy
            other = jnp.where(other >= 4, other - 4, other)
            base = form + lax.div(j, 4)
            for dz in (4, 3, 5, 2, 6, 1, 7, 0):
                group = base + 8 * dz
                group = jnp.where(group >= 64, group - 64, group)

                def go():
                    pltpu.make_async_remote_copy(
                        src_ref=send.at[c, group * 4 + other],
                        dst_ref=out_hbm.at[c, me],
                        send_sem=send_sem,
                        recv_sem=recv_sem,
                        device_id=(group, other),
                        device_id_type=MESH,
                    ).start()

                if dz == 0:
                    pl.when(j > 0)(go)
                else:
                    go()
            return 0

        lax.fori_loop(0, 32, sends, 0)
        return 0

    lax.fori_loop(0, CHUNKS, chunk, 0)
    if not talk:
        copy = pltpu.make_async_copy(send, out_hbm, own_sem)
        copy.start()
        copy.wait()
        return
    pltpu.make_async_copy(send.at[:, 0], out_hbm.at[:, 0], own_sem).wait()
    pltpu.make_async_copy(send.at[:, pl.ds(0, 255)], out_hbm.at[:, pl.ds(0, 255)], send_sem).wait()
    pltpu.make_async_copy(send.at[:, pl.ds(0, 255)], out_hbm.at[:, pl.ds(0, 255)], recv_sem).wait()


def corner_turned(echoes, rate, shift, range_phase, talk=True):
    x = echoes.reshape(2, CHUNKS * LINES, R1, R2)
    rp = range_phase.reshape(R2, R1).T * (1.0 / TWO_PI)
    vmem = pl.BlockSpec(memory_space=pltpu.VMEM)
    smem = pl.BlockSpec(memory_space=pltpu.SMEM)
    hbm = pl.BlockSpec(memory_space=pl.ANY)
    return pl.pallas_call(
        functools.partial(range_kernel, talk=talk),
        out_shape=jax.ShapeDtypeStruct((CHUNKS, 256, 2 * LINES, R2), BF16),
        in_specs=[hbm, smem, smem] + [vmem] * 7,
        out_specs=hbm,
        scratch_shapes=[
            pltpu.VMEM((CHUNKS, 2, LINES, R1, R2), BF16),
            pltpu.VMEM((LINES, 2, R1, R2), BF16),
            pltpu.VMEM((CHUNKS, 256, 2 * LINES, R2), BF16),
            pltpu.SemaphoreType.DMA((CHUNKS,)),
            pltpu.SemaphoreType.DMA,
            pltpu.SemaphoreType.DMA,
            pltpu.SemaphoreType.DMA,
        ],
        compiler_params=pltpu.CompilerParams(has_side_effects=True, vmem_limit_bytes=48 * 2**20),
        cost_estimate=pl.CostEstimate(flops=7 * 10**9, bytes_accessed=10**7, transcendentals=0),
        name="range_lines",
    )(x, rate, shift, rp, *[jnp.asarray(t) for t in range_tables()])


def azimuth_kernel(
    r_hbm, first_hbm, middle_hbm, third_hbm, second, fourth, rate, sel, centers, img_hbm, terms,
    r, y, z, first, middle, third, img, sems, tab_sems, out_sem,
):
    loads = [
        pltpu.make_async_copy(r_hbm.at[pl.ds(2 * h, 2)], r.at[pl.ds(2 * h, 2)], sems.at[h])
        for h in range(2)
    ]
    tables = [
        pltpu.make_async_copy(a, b, tab_sems.at[i])
        for i, (a, b) in enumerate([(first_hbm, first), (middle_hbm, middle), (third_hbm, third)])
    ]
    tables[0].start()
    loads[0].start()
    loads[1].start()
    tables[1].start()
    tables[2].start()

    def pair_of(ref, h, *index):
        return jnp.concatenate([ref[(2 * h + i, *index)].reshape(256, R2) for i in range(2)], axis=1)

    def forward(wait):
        for h in range(2):
            if wait:
                if h == 0:
                    tables[0].wait()
                loads[h].wait()

            def one(s, _):
                out = dot(first[s], pair_of(r, h, slice(None), s)).astype(BF16)
                for i in range(2):
                    y[2 * h + i, :, s] = out[:, R2 * i : R2 * i + R2].reshape(16, 16, R2)
                return 0

            lax.fori_loop(0, 16, one, 0, unroll=4)
        for h in range(2):

            def two(k, _):
                out = dot(second[...], pair_of(y, h, k)).astype(BF16)
                for i in range(2):
                    z[:, k, 2 * h + i] = out[:, R2 * i : R2 * i + R2].reshape(16, 16, R2)
                return 0

            lax.fori_loop(0, 16, two, 0, unroll=4)

    nothing = jnp.zeros((64, R2), BF16)

    def spectrum(k):
        k2, k1 = lax.div(k, 16), lax.rem(k, 16)
        v = dot(middle[k], jnp.concatenate([z[k2, k1].reshape(64, R2), nothing], axis=0))
        return v[:32], v[32:]

    forward(True)
    tables[1].wait()
    m = lax.broadcasted_iota(jnp.int32, (32, R2), 0)
    m = jnp.where(m >= 16, m - 32, m).astype(F32) * (1.0 / 32)
    cycles = rate[...] * (1.0 / TWO_PI)

    def filtered(k, _):
        re, im = spectrum(k)
        f = m + k.astype(F32) * (1.0 / AZ)
        cosine, sine = cos_sin(f * f * cycles)
        history = jnp.concatenate(
            [
                nothing,
                (re * cosine + im * sine).astype(BF16),
                (im * cosine - re * sine).astype(BF16),
            ],
            axis=0,
        )
        z[lax.div(k, 16), lax.rem(k, 16)] = dot(middle[k], history).astype(BF16).reshape(4, 16, R2)
        return 0

    lax.fori_loop(0, 256, filtered, 0, unroll=8)
    tables[2].wait()
    for h in range(2):

        def three(k, _):
            out = jnp.concatenate([z[:, k, 2 * h + i].reshape(256, R2) for i in range(2)], axis=1)
            out = dot(third[k], out).astype(BF16)
            for i in range(2):
                y[2 * h + i, :, k] = out[:, R2 * i : R2 * i + R2].reshape(16, 16, R2)
            return 0

        lax.fori_loop(0, 16, three, 0, unroll=4)
    for h in range(2):

        def four(s, _):
            out = dot(fourth[...], pair_of(y, h, s))
            out = out.reshape(16, 2, LINES, 2 * R2)
            out = jnp.concatenate([out[..., :R2], out[..., R2:]], axis=2).astype(BF16)
            for a in range(2):
                img[a, :, s, 16 * h : 16 * h + 16] = out[:, a]
            return 0

        lax.fori_loop(0, 16, four, 0, unroll=4)
    image_out = pltpu.make_async_copy(img, img_hbm, out_sem)
    image_out.start()

    line = lax.broadcasted_iota(jnp.int32, (256, R2), 0)

    def windowed(t, _):
        hi, lo = lax.div(t, 2), lax.rem(t, 2) * 8
        away = jnp.bitwise_and(line + 256 * t - centers[...], AZ - 1)
        away = jnp.minimum(away, AZ - away).astype(F32)
        window = jnp.maximum(1.0 - away * (16.0 / AZ), 0.0)
        parts = [
            (dot(img[a, hi, pl.ds(lo, 8)].reshape(256, R2), sel[...]) * window).reshape(8, 4, 1, LINES, R2)
            for a in range(2)
        ]
        both = jnp.concatenate(parts, axis=2).astype(BF16)
        for c in range(CHUNKS):
            r[c, hi, pl.ds(lo, 8)] = both[:, c].reshape(8, 16, R2)
        return 0

    lax.fori_loop(0, 32, windowed, 0, unroll=2)
    forward(False)

    first_re, first_im = spectrum(0)
    end_re, end_im = pltpu.roll(first_re, 31, 0), pltpu.roll(first_im, 31, 0)

    def group(g, carry):
        re, im = carry
        cross = jnp.zeros((32, R2), F32)
        energy = jnp.zeros((32, R2), F32)
        for i in range(32):
            k = g * 32 + i + 1
            if i < 31:
                next_re, next_im = spectrum(k)
            else:
                next_re, next_im = spectrum(lax.rem(k, 256))
                next_re = jnp.where(g == 7, end_re, next_re)
                next_im = jnp.where(g == 7, end_im, next_im)
            cross += re * next_im - im * next_re
            energy += re * re + im * im
            re, im = next_re, next_im
        terms[0, g] = cross
        terms[1, g] = energy
        return re, im

    lax.fori_loop(0, 8, group, (first_re, first_im))
    image_out.wait()


def focused(arrived, rate, sel, centers):
    vmem = pl.BlockSpec(memory_space=pltpu.VMEM)
    hbm = pl.BlockSpec(memory_space=pl.ANY)
    first, second, middle, third, fourth = [jnp.asarray(t) for t in azimuth_tables()]
    image, terms = pl.pallas_call(
        azimuth_kernel,
        out_shape=(
            jax.ShapeDtypeStruct((2, 16, 16, 32, R2), BF16),
            jax.ShapeDtypeStruct((2, 8, 32, R2), F32),
        ),
        in_specs=[hbm] * 4 + [vmem] * 5,
        out_specs=(hbm, vmem),
        scratch_shapes=[
            pltpu.VMEM((4, 16, 16, 16, R2), BF16),
            pltpu.VMEM((4, 16, 16, 16, R2), BF16),
            pltpu.VMEM((16, 16, 4, 16, R2), BF16),
            pltpu.VMEM((16, 256, 256), BF16),
            pltpu.VMEM((256, 64, 128), BF16),
            pltpu.VMEM((16, 256, 256), BF16),
            pltpu.VMEM((2, 16, 16, 32, R2), BF16),
            pltpu.SemaphoreType.DMA((2,)),
            pltpu.SemaphoreType.DMA((3,)),
            pltpu.SemaphoreType.DMA,
        ],
        compiler_params=pltpu.CompilerParams(vmem_limit_bytes=56 * 2**20),
        cost_estimate=pl.CostEstimate(flops=15 * 10**9, bytes_accessed=2 * 10**7, transcendentals=0),
        name="azimuth_columns",
    )(arrived.reshape(4, 16, 16, 16, R2), first, middle, third, second, fourth, rate[None], sel, centers)
    return image.reshape(2, AZ, R2), terms


def on_device(
    echoes,
    scale_rate,
    migration,
    range_phase,
    azimuth_rate,
    bright_columns,
    line_block,
    line_center,
):
    arrived = corner_turned(echoes, scale_rate, migration, range_phase)
    local_cols = bright_columns[0] - lax.axis_index("focus") * R2
    spare = (0, R2 - local_cols.shape[0])
    local_cols = jnp.pad(local_cols, spare, constant_values=-1)
    sel = (jnp.arange(R2, dtype=jnp.int32)[:, None] == local_cols[None, :]).astype(BF16)
    centers = jnp.pad(line_center[0], spare)[None]
    blocks = jnp.pad(line_block[0, :, 0], spare, constant_values=-1)
    focused_image, terms = focused(arrived, azimuth_rate, sel, centers)
    onehot = (jnp.arange(NBLK, dtype=jnp.int32)[:, None] == blocks[None, :]).astype(F32)
    partial_maps = jnp.einsum(
        "bl,sgml->bsgm", onehot, terms, precision=lax.Precision.HIGHEST
    )
    own_rows = lax.all_to_all(
        partial_maps.reshape(NBLK, 2, 256), ("form", "focus"), split_axis=0, concat_axis=0, tiled=True
    ).sum(axis=0)
    own_map = own_rows[0] / (own_rows[1] + EPSILON)
    phase_map = own_map.reshape(8, 32).T.reshape(1, 256)
    return (focused_image, phase_map)


def solution(mesh):
    in_specs = (
        P(None, ("form", "focus"), None),
        P(("form", "focus")),
        P(("form", "focus")),
        P(),
        P(("form", "focus")),
        P("form", None),
        P("form", None, None),
        P("form", None),
    )
    out_specs = (P(None, None, ("form", "focus")), P(("form", "focus"), None))
    return jax.shard_map(
        on_device, mesh=mesh, in_specs=in_specs, out_specs=out_specs, check_vma=False
    )
```

profile of v0, /device:TPU:1, one launch (start us, length us, event | category | flops | bytes accessed | tf_op | source)
XLA Modules:
  0.0 251.5 jit_solution(7773504036025604234)
XLA Ops:
  0.6 0.0 copy-start.8
  0.6 0.0 copy-start.9
  0.7 0.0 copy-start.10
  0.7 0.0 copy-start.11
  0.7 0.0 copy-start
  0.7 0.0 copy-start.1
  0.7 0.0 copy-start.2
  0.7 0.0 copy-start.3
  0.7 0.0 copy-start.4
  0.7 0.0 copy-start.5
  0.7 0.0 copy-start.6
  0.8 0.0 copy-start.7
  0.8 5.5 %copy.27 = bf16[8,8,256,128]{3,2,1,0:T(8,128)(2,1)} copy(bf16[8,8,256,128]{3,1,2,0:T(8,128)(2,1)} %bitcast.23) | data formatting | bytes 8388608
  6.3 0.0 copy-done.8
  6.3 0.1 copy.23
  6.4 0.0 copy-done.9
  6.5 0.6 fusion.4.sel
  7.1 0.0 copy-done.10
  7.1 0.5 pad_bitcast_fusion.centers
  7.6 0.0 copy-done.11
  7.6 0.0 copy-done
  7.6 0.0 copy-done.1
  7.6 0.0 copy-done.2
  7.7 122.5 %range_lines.1 = bf16[4,256,16,128]{3,2,1,0:T(8,128)(2,1)} custom-call(bf16[2,32,256,128]{3,2,1,0:T(8,128)(2,1)} %bitcast.24, f32[32]{0:T(128)S(1)} %copy-done, f32[32]{0:T(128)S(1)} %copy-done.1, f32[256,128]{1,0:T(8,128)S(1)} %bitcast.22, bf16[512,512]{1,0:T(8,128)(2,1)S(1)} %copy-done.2, bf16[256,256]{1,0:T(8,128)(2,1)S(1)} %copy-done.5, ...), custom_call_target="tpu_custom_call" | custom-call | flops 7000000000 | bytes 10000000 | tf_op jit(solution)/shard_map/range_lines/pallas_call | solution.py:229
  130.2 92.6 %azimuth_columns.1 = (bf16[2,16,16,32,128]{4,3,2,1,0:T(8,128)(2,1)}, f32[2,8,32,128]{3,2,1,0:T(8,128)}) custom-call(bf16[4,16,16,16,128]{4,3,2,1,0:T(8,128)(2,1)} %bitcast.31, bf16[16,256,256]{2,1,0:T(8,128)(2,1)} %constant.44.clone.first_hbm, bf16[256,64,128]{2,1,0:T(8,128)(2,1)} %constant.46.clone.middle_hbm, ...), custom_call_target="tpu_custom_call" | custom-call | flops 15000000512 | bytes 20000000 | tf_op jit(solution)/shard_map/azimuth_columns/pallas_call | solution.py:397
  222.9 1.3 fusion.1
  224.2 0.2 copy.24
  224.4 26.0 %all_to_all.5 = f32[256,2,256]{2,1,0:T(2,128)S(1)} all-to-all(f32[256,2,256]{2,1,0:T(2,128)S(1)} %copy.24), channel_id=1, replica_groups=mesh['form'=64,'focus'=4] {'form','focus'}, dimensions={0} | all-to-all | bytes 1048576 | tf_op jit(solution)/shard_map/all_to_all | solution.py:446
  250.4 0.3 reduce_sum.9
  250.7 0.1 div.8
  250.8 0.1 copy.25
  250.9 0.7 reshape.36
  (11 shorter events, 0.1 us)
Async XLA Ops:
  0.6 5.6 %copy-start.8 = (f32[32768]{0:T(1024)S(1)}, f32[32768]{0:T(1024)}, u32[]{:S(2)}) copy-start(f32[32768]{0:T(1024)} %param.22) | copy-start | bytes 393220
  0.6 5.8 %copy-start.9 = (s32[1,32]{1,0:T(1,128)S(1)}, s32[1,32]{1,0:T(1,128)}, u32[]{:S(2)}) copy-start(s32[1,32]{1,0:T(1,128)} %param.24) | copy-start | bytes 388
  0.7 6.4 %copy-start.10 = (s32[1,32]{1,0:T(1,128)S(1)}, s32[1,32]{1,0:T(1,128)}, u32[]{:S(2)}) copy-start(s32[1,32]{1,0:T(1,128)} %param.26) | copy-start | bytes 388
  0.7 6.9 %copy-start.11 = (s32[1,32,1]{1,2,0:T(1,128)S(1)}, s32[1,32,1]{1,2,0:T(1,128)}, u32[]{:S(2)}) copy-start(s32[1,32,1]{1,2,0:T(1,128)} %param.25) | copy-start | bytes 388
  0.7 6.9 %copy-start = (f32[32]{0:T(128)S(1)}, f32[32]{0:T(128)}, u32[]{:S(2)}) copy-start(f32[32]{0:T(128)} %rate.1) | copy-start | bytes 388
  0.7 6.9 %copy-start.1 = (f32[32]{0:T(128)S(1)}, f32[32]{0:T(128)}, u32[]{:S(2)}) copy-start(f32[32]{0:T(128)} %shift.1) | copy-start | bytes 388
  0.7 6.9 %copy-start.2 = (bf16[512,512]{1,0:T(8,128)(2,1)S(1)}, bf16[512,512]{1,0:T(8,128)(2,1)}, u32[]{:S(2)}) copy-start(bf16[512,512]{1,0:T(8,128)(2,1)} %constant.38.clone.first) | copy-start | bytes 1572868
  0.7 6.9 %copy-start.3 = (bf16[512,512]{1,0:T(8,128)(2,1)S(1)}, bf16[512,512]{1,0:T(8,128)(2,1)}, u32[]{:S(2)}) copy-start(bf16[512,512]{1,0:T(8,128)(2,1)} %constant.41.clone.last) | copy-start | bytes 1572868
  0.7 6.9 %copy-start.4 = (f32[4,256,128]{2,1,0:T(8,128)S(1)}, f32[4,256,128]{2,1,0:T(8,128)}, u32[]{:S(2)}) copy-start(f32[4,256,128]{2,1,0:T(8,128)} %constant.43.clone.planes) | copy-start | bytes 1572868
  0.7 6.9 %copy-start.5 = (bf16[256,256]{1,0:T(8,128)(2,1)S(1)}, bf16[256,256]{1,0:T(8,128)(2,1)}, u32[]{:S(2)}) copy-start(bf16[256,256]{1,0:T(8,128)(2,1)} %constant.39.clone.inner) | copy-start | bytes 393220
  0.7 6.9 %copy-start.6 = (bf16[256,256]{1,0:T(8,128)(2,1)S(1)}, bf16[256,256]{1,0:T(8,128)(2,1)}, u32[]{:S(2)}) copy-start(bf16[256,256]{1,0:T(8,128)(2,1)} %constant.40.clone.outer) | copy-start | bytes 393220
  0.8 6.9 %copy-start.7 = (bf16[256,256]{1,0:T(8,128)(2,1)S(1)}, bf16[256,256]{1,0:T(8,128)(2,1)}, u32[]{:S(2)}) copy-start(bf16[256,256]{1,0:T(8,128)(2,1)} %constant.42.clone.swap) | copy-start | bytes 393220
where the time goes:
time: 252 us
  Pallas kernels  215 us (85%)
  blocking collectives  26 us (10%)
  local copies, waits for them, and re-layouts  7.27 us (3%)
    pallas_call x1, Pallas kernels, corner_turned(): pl.pallas_call(functools.partial(range_kernel, talk=talk), out_shape=jax....  123 us
    pallas_call x1, Pallas kernels, focused(): pl.pallas_call(azimuth_kernel, out_shape=(jax.ShapeDtypeStruct((2, 16, 16...  92.6 us
    all_to_all x1, blocking collectives, on_device(): lax.all_to_all(partial_maps.reshape(NBLK, 2, 256), ('form', 'focus'), spl...  26 us
    unnamed x25, local copies, waits for them, and re-layouts  5.57 us

commit v1 on v0

v1 whole, which is shorter than its diff:
```python
import functools
import math

import jax
import jax.numpy as jnp
import ml_dtypes
import numpy as np
from jax import lax
from jax.experimental import pallas as pl
from jax.experimental.pallas import tpu as pltpu
from jax.sharding import PartitionSpec as P

R1 = 256
R2 = 128
NBLK = 256
AZ = 8192
CHUNKS = 4
LISTED = 32
LINES = 8
MESH = pl.DeviceIdType.MESH
F32 = jnp.float32
BF16 = jnp.bfloat16

TWO_PI = 2.0 * math.pi
EPSILON = 1e-06


def real_blocks(values):
    upper = np.stack([values.real, -values.imag], axis=-2)
    lower = np.stack([values.imag, values.real], axis=-2)
    return np.stack([upper, lower], axis=-4)


def unit(turns):
    return np.exp(2j * np.pi * turns)


def range_tables():
    k = np.arange(R1)
    n = np.arange(R2)
    wide = np.outer(k, k) % R1 / R1
    narrow = np.outer(n, n) % R2 / R2
    first = real_blocks(unit(-wide) / 16).reshape(2 * R1, 2 * R1)
    last = real_blocks(unit(wide) / 16).reshape(2 * R1, 2 * R1)
    inner = real_blocks(unit(-narrow) / math.sqrt(R2)).reshape(2 * R2, 2 * R2).T
    outer = real_blocks(unit(narrow) / math.sqrt(R2)).reshape(2 * R2, 2 * R2).T
    twist = unit(np.outer(k, n) / (R1 * R2))
    length = R1 * R2
    offsets = (k[:, None] * R2 + n[None, :] - length // 2) / length
    bins = k[:, None] + R1 * n[None, :]
    signed = np.where(bins >= length // 2, bins - length, bins) / length
    planes = np.stack([twist.real, twist.imag, offsets * offsets / TWO_PI, signed])
    swap = np.eye(256).reshape(LINES, 2, 16, 256).transpose(2, 1, 0, 3).reshape(256, 256)
    cross = np.eye(256).reshape(16, 16, 256).transpose(1, 0, 2).reshape(256, 256)
    half = [t.astype(ml_dtypes.bfloat16) for t in (first, inner, outer, last, swap, cross)]
    return half + [planes.astype(np.float32)]


def azimuth_tables():
    i = np.arange(16)
    near = np.outer(i, i) / 16
    shift = np.outer(i, i) / 256
    l8, m = np.arange(LINES), np.arange(32)
    eye = np.eye(LINES)

    def widened(turns):
        blocks = real_blocks(np.moveaxis(unit(turns) / 4, -1, 0))
        full = np.einsum("l...atcf,lm->...talfcm", blocks, eye)
        return full.reshape(*full.shape[:-6], 256, 256)

    same = np.zeros(LINES)
    lines = LINES * np.arange(CHUNKS)[:, None] + l8
    first = widened(-(near[None] + shift[:, :, None])[..., None] - same)
    second = widened(-near[None, :, :, None] - (i[:, None] * lines[:, None, :] / 512)[:, :, None, :])
    part = (lines[None] * i[:, None, None] / AZ)[:, None] + (lines * m[:, None, None] / 32)[None]
    wide = real_blocks((unit(-part) / math.sqrt(32)).reshape(16, 32, 32)).reshape(16, 2, 32, 2, CHUNKS, LINES)
    third = np.einsum("kamchl,xy->kxamyhcl", wide, np.eye(4)).reshape(16, 256, 256)
    wide = real_blocks((unit(part) / math.sqrt(32)).transpose(0, 2, 3, 1).reshape(16, 32, 32))
    wide = wide.reshape(16, 2, CHUNKS, LINES, 2, 32)
    fourth = np.einsum("kahlcm,xy->kxhalycm", wide, np.eye(4)).reshape(16, 256, 256)
    fifth = widened(near[None, :, :, None] + (i[:, None] * lines[:, None, :] / 512)[:, None, :, :])
    sixth = widened((near[None] + shift[:, None, :])[..., None] + same)
    return [t.astype(ml_dtypes.bfloat16) for t in (first, second, third, fourth, fifth, sixth)]


def cos_sin(turns):
    rest = turns - jnp.round(turns)
    z = rest * rest
    sine = rest * (6.28316395 + z * (-10.3342826 + z * (5.08377413 - 1.1092177 * z)))
    cosine = 0.99999995 + z * (-4.93479283 + z * (4.05841135 + z * (-1.33187657 + 0.21968961 * z)))
    return 1.0 - 0.5 * (sine * sine), sine * cosine


def dot(a, b):
    return jnp.dot(a, b, preferred_element_type=F32)


def range_kernel(
    x_hbm, rate, shift, phase, *args, talk=True,
):
    sources, out_hbm, tables = args[:7], args[7], args[8:15]
    raw, xbuf, rp, rows, send, in_sem, tab_sem, send_sem, recv_sem, own_sem = args[15:]
    first, inner, outer, last, swap, cross, planes = tables
    loads = [
        pltpu.make_async_copy(x_hbm.at[:, pl.ds(16 * h, 16)], raw.at[h], in_sem.at[h]) for h in range(2)
    ]
    copies = [pltpu.make_async_copy(a, b, tab_sem.at[i]) for i, (a, b) in enumerate(zip(sources, tables))]
    loads[0].start()
    for i in (5, 6, 0, 1, 2, 3, 4):
        copies[i].start()
    loads[1].start()
    rp[...] = phase[...].T * (1.0 / TWO_PI)
    copies[5].wait()
    if talk:
        form = lax.axis_index("form")
        focus = lax.axis_index("focus")
        me = form * 4 + focus
        barrier = pltpu.get_barrier_semaphore()

        def greet(j, _):
            for d in range(8):
                group = form + j + 8 * d
                group = jnp.where(group >= 64, group - 64, group)
                for dy in range(4):
                    other = focus + dy
                    other = jnp.where(other >= 4, other - 4, other)

                    def hello():
                        pl.semaphore_signal(
                            barrier, inc=1, device_id=(group, other), device_id_type=MESH
                        )

                    if d == 0 and dy == 0:
                        pl.when(j > 0)(hello)
                    else:
                        hello()
            return 0

        lax.fori_loop(0, 8, greet, 0)

    def chunk(c, _):
        h = lax.div(c, 2)

        @pl.when(lax.rem(c, 2) == 0)
        def _():
            pltpu.make_async_copy(x_hbm.at[:, pl.ds(16 * h, 16)], raw.at[h], in_sem.at[h]).wait()

            def unfold(t, _):
                cut = [
                    jnp.concatenate(
                        [
                            raw[h, a, :, pl.ds(pl.multiple_of(2048 * t + R2 * i, R2), R2)]
                            for i in range(16)
                        ],
                        axis=0,
                    )
                    for a in range(2)
                ]
                out = dot(cross[...], jnp.concatenate(cut, axis=1)).astype(BF16)
                for a in range(2):
                    xbuf[a, :, pl.ds(pl.multiple_of(16 * t, 16), 16)] = out[
                        :, R2 * a : R2 * a + R2
                    ].reshape(16, 16, R2)
                return 0

            lax.fori_loop(0, 16, unfold, 0, unroll=4)

        @pl.when(c == 0)
        def _():
            for i in (6, 0, 1, 2, 3, 4):
                copies[i].wait()

        half = LINES * lax.rem(c, 2)

        def two_lines(p, _):
            parts = []
            for i in range(2):
                l = 2 * p + i
                cosine, sine = cos_sin(rate[LINES * c + l] * planes[2])
                re = xbuf[0, half + l].astype(F32)
                im = xbuf[1, half + l].astype(F32)
                parts.append(
                    jnp.concatenate(
                        [
                            (re * cosine - im * sine).astype(BF16),
                            (re * sine + im * cosine).astype(BF16),
                        ],
                        axis=0,
                    )
                )
            u = dot(first[...], jnp.concatenate(parts, axis=1))
            parts = []
            for i in range(2):
                lanes = slice(R2 * i, R2 * i + R2)
                re, im = u[:R1, lanes], u[R1:, lanes]
                cosine, sine = planes[0], planes[1]
                twisted = jnp.concatenate(
                    [
                        (re * cosine + im * sine).astype(BF16),
                        (im * cosine - re * sine).astype(BF16),
                    ],
                    axis=1,
                )
                spectrum = dot(twisted, inner[...])
                re, im = spectrum[:, :R2], spectrum[:, R2:]
                cosine, sine = cos_sin(rp[...] + shift[LINES * c + 2 * p + i] * planes[3])
                matched = jnp.concatenate(
                    [
                        (re * cosine + im * sine).astype(BF16),
                        (im * cosine - re * sine).astype(BF16),
                    ],
                    axis=1,
                )
                w = dot(matched, outer[...])
                re, im = w[:, :R2], w[:, R2:]
                cosine, sine = planes[0], planes[1]
                parts.append(
                    jnp.concatenate(
                        [
                            (re * cosine - im * sine).astype(BF16),
                            (re * sine + im * cosine).astype(BF16),
                        ],
                        axis=0,
                    )
                )
            done = dot(last[...], jnp.concatenate(parts, axis=1)).astype(BF16)
            for i in range(2):
                for a in range(2):
                    rows[2 * p + i, a] = done[R1 * a : R1 * a + R1, R2 * i : R2 * i + R2]
            return 0

        lax.fori_loop(0, LINES // 2, two_lines, 0, unroll=4)

        def swapped(t, _):
            cut = [
                rows[:, :, pl.ds(pl.multiple_of(32 * t + 16 * i, 16), 16)].reshape(256, R2)
                for i in range(2)
            ]
            out = dot(swap[...], jnp.concatenate(cut, axis=1)).astype(BF16)
            for i in range(2):
                send[c, pl.ds(32 * t + 16 * i, 16)] = out[:, R2 * i : R2 * i + R2].reshape(16, 16, R2)
            return 0

        lax.fori_loop(0, 8, swapped, 0, unroll=2)
        if not talk:
            return 0

        @pl.when(c == 0)
        def _():
            pl.semaphore_wait(barrier, 255)

        pltpu.make_async_copy(send.at[c, me], out_hbm.at[c, me], own_sem).start()

        def sends(j, _):
            dy = lax.rem(j, 4)
            other = focus + dy
            other = jnp.where(other >= 4, other - 4, other)
            base = form + lax.div(j, 4)
            for dz in (4, 3, 5, 2, 6, 1, 7, 0):
                group = base + 8 * dz
                group = jnp.where(group >= 64, group - 64, group)

                def go():
                    pltpu.make_async_remote_copy(
                        src_ref=send.at[c, group * 4 + other],
                        dst_ref=out_hbm.at[c, me],
                        send_sem=send_sem,
                        recv_sem=recv_sem,
                        device_id=(group, other),
                        device_id_type=MESH,
                    ).start()

                if dz == 0:
                    pl.when(j > 0)(go)
                else:
                    go()
            return 0

        lax.fori_loop(0, 32, sends, 0)
        return 0

    lax.fori_loop(0, CHUNKS, chunk, 0)
    if not talk:
        copy = pltpu.make_async_copy(send, out_hbm, own_sem)
        copy.start()
        copy.wait()
        return
    pltpu.make_async_copy(send.at[:, 0], out_hbm.at[:, 0], own_sem).wait()
    pltpu.make_async_copy(send.at[:, pl.ds(0, 255)], out_hbm.at[:, pl.ds(0, 255)], send_sem).wait()
    pltpu.make_async_copy(send.at[:, pl.ds(0, 255)], out_hbm.at[:, pl.ds(0, 255)], recv_sem).wait()


def corner_turned(echoes, rate, shift, range_phase, talk=True):
    phase = range_phase.reshape(R2, R1)
    tables = range_tables()
    vmem = pl.BlockSpec(memory_space=pltpu.VMEM)
    smem = pl.BlockSpec(memory_space=pltpu.SMEM)
    hbm = pl.BlockSpec(memory_space=pl.ANY)
    return pl.pallas_call(
        functools.partial(range_kernel, talk=talk),
        out_shape=jax.ShapeDtypeStruct((CHUNKS, 256, 2 * LINES, R2), BF16),
        in_specs=[hbm, smem, smem, vmem] + [hbm] * 7,
        out_specs=hbm,
        scratch_shapes=[
            *[pltpu.VMEM(t.shape, t.dtype) for t in tables],
            pltpu.VMEM((2, 2, 16, R1 * R2), BF16),
            pltpu.VMEM((2, 16, R1, R2), BF16),
            pltpu.VMEM((R1, R2), F32),
            pltpu.VMEM((LINES, 2, R1, R2), BF16),
            pltpu.VMEM((CHUNKS, 256, 2 * LINES, R2), BF16),
            pltpu.SemaphoreType.DMA((2,)),
            pltpu.SemaphoreType.DMA((7,)),
            pltpu.SemaphoreType.DMA,
            pltpu.SemaphoreType.DMA,
            pltpu.SemaphoreType.DMA,
        ],
        compiler_params=pltpu.CompilerParams(
            has_side_effects=True, vmem_limit_bytes=62 * 2**20, **({"collective_id": 0} if talk else {})
        ),
        cost_estimate=pl.CostEstimate(flops=7 * 10**9, bytes_accessed=10**7, transcendentals=0),
        name="range_lines",
    )(echoes, rate, shift, phase, *[jnp.asarray(t) for t in tables])


def azimuth_kernel(
    r_hbm, t1, t2, t3, t4, t5, t6, rate, listed, held, img_hbm, terms,
    r, y, z, back, v, first, second, third, fourth, fifth, sixth, img, sums, sel, centers, sems, tab_sems, out_sem, *, split=True,
):
    loads = [
        pltpu.make_async_copy(r_hbm.at[pl.ds(2 * h, 2)], r.at[pl.ds(2 * h, 2)], sems.at[h])
        for h in range(2)
    ]
    tables = [
        pltpu.make_async_copy(a, b, tab_sems.at[i])
        for i, (a, b) in enumerate(
            [(t1, first), (t2, second), (t3, third), (t4, fourth), (t5, fifth), (t6, sixth)]
        )
    ]
    tables[0].start()
    loads[0].start()
    loads[1].start()
    for i in range(1, 6):
        tables[i].start()

    own = lax.axis_index("focus") * R2 if split else 0
    centers[...] = jnp.zeros((2, R2), jnp.int32) - 1
    centers[0:1, :LISTED] = held[...]
    centers[1:2, :LISTED] = listed[...] - own
    column = lax.broadcasted_iota(jnp.int32, (R2, R2), 0)
    sel[...] = jnp.where(column == centers[1:2], 1.0, 0.0).astype(BF16)

    def pair(one, other):
        return jnp.concatenate([one.reshape(256, R2), other.reshape(256, R2)], axis=1)

    def halves(out):
        out = out.astype(BF16)
        return [out[:, R2 * i : R2 * i + R2].reshape(16, 16, R2) for i in range(2)]

    def forward(wait):
        for h in range(2):
            if wait:
                if h == 0:
                    tables[0].wait()
                loads[h].wait()

            def one(s, _):
                out = halves(dot(first[s], pair(r[2 * h, :, s], r[2 * h + 1, :, s])))
                for i in range(2):
                    y[2 * h + i, :, s] = out[i]
                return 0

            lax.fori_loop(0, 16, one, 0, unroll=4)
        if wait:
            tables[1].wait()
        for c in range(CHUNKS):

            def two(k, _):
                out = halves(dot(second[c], pair(y[c, 2 * k], y[c, 2 * k + 1])))
                for i in range(2):
                    z[:, 2 * k + i, c] = out[i]
                return 0

            lax.fori_loop(0, 8, two, 0, unroll=4)

    def spectrum(k, h):
        return dot(third[k], pair(z[pl.ds(8 * h, 4), k], z[pl.ds(8 * h + 4, 4), k]))

    forward(True)
    for i in range(2, 6):
        tables[i].wait()
    m = lax.broadcasted_iota(jnp.int32, (32, R2), 0)
    m = jnp.where(m >= 16, m - 32, m).astype(F32) * (1.0 / 32)
    cycles = rate[...] * (1.0 / TWO_PI)

    def filtered(j, _):
        k, h = lax.div(j, 2), lax.rem(j, 2)
        out = spectrum(k, h)
        columns = []
        for i in range(2):
            rows = []
            for x in range(4):
                re = out[64 * x : 64 * x + 32, R2 * i : R2 * i + R2]
                im = out[64 * x + 32 : 64 * x + 64, R2 * i : R2 * i + R2]
                f = m + (k + 16 * (8 * h + 4 * i + x)).astype(F32) * (1.0 / AZ)
                cosine, sine = cos_sin(f * f * cycles)
                rows.append((re * cosine + im * sine).astype(BF16))
                rows.append((im * cosine - re * sine).astype(BF16))
            columns.append(jnp.concatenate(rows, axis=0))
        out = dot(fourth[k], jnp.concatenate(columns, axis=1)).astype(BF16)
        for i in range(2):
            back[pl.ds(8 * h + 4 * i, 4), k] = out[:, R2 * i : R2 * i + R2].reshape(4, 4, 16, R2)
        return 0

    lax.fori_loop(0, 32, filtered, 0, unroll=2)
    for c in range(CHUNKS):

        def three(k, _):
            out = halves(dot(fifth[c], pair(back[:, 2 * k, c], back[:, 2 * k + 1, c])))
            for i in range(2):
                y[c, :, 2 * k + i] = out[i]
            return 0

        lax.fori_loop(0, 8, three, 0, unroll=4)
    for h in range(2):

        def four(s, _):
            out = dot(sixth[s], pair(y[2 * h, s], y[2 * h + 1, s]))
            out = out.reshape(16, 2, LINES, 2 * R2)
            out = jnp.concatenate([out[..., :R2], out[..., R2:]], axis=2).astype(BF16)
            for a in range(2):
                img[a, :, s, 16 * h : 16 * h + 16] = out[:, a]
            return 0

        lax.fori_loop(0, 16, four, 0, unroll=4)
    image_out = pltpu.make_async_copy(img, img_hbm, out_sem)
    image_out.start()

    line = lax.broadcasted_iota(jnp.int32, (256, R2), 0)

    def windowed(t, _):
        hi, lo = lax.div(t, 2), lax.rem(t, 2) * 8
        away = jnp.bitwise_and(line + 256 * t - centers[0:1], AZ - 1)
        away = jnp.minimum(away, AZ - away).astype(F32)
        window = jnp.maximum(1.0 - away * (16.0 / AZ), 0.0)
        parts = [
            (dot(img[a, hi, pl.ds(lo, 8)].reshape(256, R2), sel[...]) * window).reshape(8, 4, 1, LINES, R2)
            for a in range(2)
        ]
        both = jnp.concatenate(parts, axis=2).astype(BF16)
        for c in range(CHUNKS):
            r[c, hi, pl.ds(lo, 8)] = both[:, c].reshape(8, 16, R2)
        return 0

    lax.fori_loop(0, 32, windowed, 0, unroll=2)
    forward(False)

    def line_spectrum(j, _):
        k, h = lax.div(j, 2), lax.rem(j, 2)
        out = spectrum(k, h)
        for i in range(2):
            v[pl.ds(8 * h + 4 * i, 4), k] = out[:, R2 * i : R2 * i + R2].reshape(4, 2, 32, R2)
        return 0

    lax.fori_loop(0, 32, line_spectrum, 0, unroll=4)
    end_re, end_im = pltpu.roll(v[0, 0, 0], 31, 0), pltpu.roll(v[0, 0, 1], 31, 0)

    def group(g, _):
        cross = jnp.zeros((32, R2), F32)
        energy = jnp.zeros((32, R2), F32)
        re, im = v[2 * g, 0, 0], v[2 * g, 0, 1]
        for i in range(1, 33):
            k2 = 2 * g + i // 16
            if i == 32:
                k2 = lax.rem(k2, 16)
            next_re, next_im = v[k2, i % 16, 0], v[k2, i % 16, 1]
            if i == 32:
                next_re = jnp.where(g == 7, end_re, next_re)
                next_im = jnp.where(g == 7, end_im, next_im)
            cross += re * next_im - im * next_re
            energy += re * re + im * im
            re, im = next_re, next_im
        sums[pl.ds(g, 32, stride=8)] = cross
        sums[pl.ds(256 + g, 32, stride=8)] = energy
        return 0

    lax.fori_loop(0, 8, group, 0)
    terms[...] = sums[...].T[:LISTED]
    image_out.wait()


def focused(arrived, rate, listed, held, split=True):
    vmem = pl.BlockSpec(memory_space=pltpu.VMEM)
    hbm = pl.BlockSpec(memory_space=pl.ANY)
    tables = azimuth_tables()
    image, terms = pl.pallas_call(
        functools.partial(azimuth_kernel, split=split),
        out_shape=(
            jax.ShapeDtypeStruct((2, 16, 16, 32, R2), BF16),
            jax.ShapeDtypeStruct((LISTED, 512), F32),
        ),
        in_specs=[hbm] * 7 + [vmem] * 3,
        out_specs=(hbm, vmem),
        scratch_shapes=[
            pltpu.VMEM((4, 16, 16, 16, R2), BF16),
            pltpu.VMEM((4, 16, 16, 16, R2), BF16),
            pltpu.VMEM((16, 16, 4, 16, R2), BF16),
            pltpu.VMEM((16, 16, 4, 16, R2), BF16),
            pltpu.VMEM((16, 16, 2, 32, R2), F32),
            *[pltpu.VMEM(t.shape, BF16) for t in tables],
            pltpu.VMEM((2, 16, 16, 32, R2), BF16),
            pltpu.VMEM((512, R2), F32),
            pltpu.VMEM((R2, R2), BF16),
            pltpu.VMEM((2, R2), jnp.int32),
            pltpu.SemaphoreType.DMA((2,)),
            pltpu.SemaphoreType.DMA((6,)),
            pltpu.SemaphoreType.DMA,
        ],
        compiler_params=pltpu.CompilerParams(vmem_limit_bytes=62 * 2**20),
        cost_estimate=pl.CostEstimate(flops=15 * 10**9, bytes_accessed=2 * 10**7, transcendentals=0),
        name="azimuth_columns",
    )(arrived.reshape(4, 16, 16, 16, R2), *[jnp.asarray(t) for t in tables], rate[None], listed, held)
    return image.reshape(2, AZ, R2), terms


def map_kernel(terms, blocks, out, got, rows, parts, send_sem, recv_sem, row_send, row_recv):
    form = lax.axis_index("form")
    focus = lax.axis_index("focus")
    barrier = pltpu.get_barrier_semaphore()
    for d in range(1, 4):
        other = focus + d
        other = jnp.where(other >= 4, other - 4, other)
        pl.semaphore_signal(barrier, inc=1, device_id=(form, other), device_id_type=MESH)

    def greet(j, _):
        for dz in range(8):
            other = form + j + 8 * dz
            other = jnp.where(other >= 64, other - 64, other)

            def hello():
                pl.semaphore_signal(barrier, inc=1, device_id=(other, focus), device_id_type=MESH)

            if dz == 0:
                pl.when(j > 0)(hello)
            else:
                hello()
        return 0

    lax.fori_loop(0, 8, greet, 0)
    own = 4 * lax.broadcasted_iota(jnp.int32, (64, LISTED), 0) + focus
    chosen = jnp.where(own == blocks[...], 1.0, 0.0)
    pl.semaphore_wait(barrier, 66)
    copies = []
    for d in range(1, 4):
        other = focus + d
        other = jnp.where(other >= 4, other - 4, other)
        copies.append(
            pltpu.make_async_remote_copy(
                src_ref=terms,
                dst_ref=got.at[d - 1],
                send_sem=send_sem.at[d - 1],
                recv_sem=recv_sem.at[d - 1],
                device_id=(form, other),
                device_id_type=MESH,
            )
        )
        copies[-1].start()
    for copy in copies:
        copy.wait_recv()
    group = terms[...] + got[0] + (got[1] + got[2])
    mine = jnp.dot(
        chosen, group, preferred_element_type=F32, precision=lax.Precision.HIGHEST
    )
    for i in range(4):
        rows[:, i] = mine[:, R2 * i : R2 * i + R2]
    parts[form] = rows[form]

    def sends(j, _):
        for dz in (4, 3, 5, 2, 6, 1, 7, 0):
            other = form + j + 8 * dz
            other = jnp.where(other >= 64, other - 64, other)

            def go():
                pltpu.make_async_remote_copy(
                    src_ref=rows.at[other],
                    dst_ref=parts.at[form],
                    send_sem=row_send,
                    recv_sem=row_recv,
                    device_id=(other, focus),
                    device_id_type=MESH,
                ).start()

            if dz == 0:
                pl.when(j > 0)(go)
            else:
                go()
        return 0

    lax.fori_loop(0, 8, sends, 0)
    for copy in copies:
        copy.wait_send()
    pltpu.make_async_copy(rows.at[pl.ds(0, 63)], parts.at[pl.ds(0, 63)], row_send).wait()
    pltpu.make_async_copy(rows.at[pl.ds(0, 63)], parts.at[pl.ds(0, 63)], row_recv).wait()
    total = jnp.sum(parts[...], axis=0)
    out[...] = total[:2] / (total[2:] + EPSILON)


def own_map(terms, blocks):
    vmem = pl.BlockSpec(memory_space=pltpu.VMEM)
    return pl.pallas_call(
        map_kernel,
        out_shape=jax.ShapeDtypeStruct((2, R2), F32),
        in_specs=[vmem, vmem],
        out_specs=vmem,
        scratch_shapes=[
            pltpu.VMEM((3, LISTED, 512), F32),
            pltpu.VMEM((64, 4, R2), F32),
            pltpu.VMEM((64, 4, R2), F32),
            pltpu.SemaphoreType.DMA((3,)),
            pltpu.SemaphoreType.DMA((3,)),
            pltpu.SemaphoreType.DMA,
            pltpu.SemaphoreType.DMA,
        ],
        compiler_params=pltpu.CompilerParams(
            has_side_effects=True, vmem_limit_bytes=62 * 2**20, collective_id=1
        ),
        name="phase_rows",
    )(terms, blocks)


def on_device(
    echoes,
    scale_rate,
    migration,
    range_phase,
    azimuth_rate,
    bright_columns,
    line_block,
    line_center,
):
    arrived = corner_turned(echoes, scale_rate, migration, range_phase)
    focused_image, terms = focused(arrived, azimuth_rate, bright_columns, line_center)
    phase_map = own_map(terms, line_block.reshape(1, LISTED)).reshape(1, 256)
    return (focused_image, phase_map)


def solution(mesh):
    in_specs = (
        P(None, ("form", "focus"), None),
        P(("form", "focus")),
        P(("form", "focus")),
        P(),
        P(("form", "focus")),
        P("form", None),
        P("form", None, None),
        P("form", None),
    )
    out_specs = (P(None, None, ("form", "focus")), P(("form", "focus"), None))
    return jax.shard_map(
        on_device, mesh=mesh, in_specs=in_specs, out_specs=out_specs, check_vma=False
    )
```

time: 252 us -> 170 us (0.67)
  Pallas kernels: 215 us -> 166 us
  blocking collectives: 26 us -> 0 us
  local copies, waits for them, and re-layouts: 7.27 us -> 2.82 us
    pallas_call x1 -> x2, Pallas kernels: 92.6 us -> 54.3 us  [the longest x1 35.8 us: focused(): pl.pallas_call(functools.partial(azimuth_kernel, split=split), out_shape=...]
    all_to_all x1 -> x0, blocking collectives: 26 us -> none  [on_device(): lax.all_to_all(partial_maps.reshape(NBLK, 2, 256), ('form', 'focus'), spl...]
    pallas_call x1, Pallas kernels: 123 us -> 112 us  [corner_turned(): pl.pallas_call(functools.partial(range_kernel, talk=talk), out_shape=jax....]
    unnamed x25 -> x1, local copies, waits for them, and re-layouts: 5.57 us -> 1.22 us
where the time goes in v1:
time: 170 us
  Pallas kernels  166 us (98%)
  local copies, waits for them, and re-layouts  2.82 us (2%)
    pallas_call x1, Pallas kernels, corner_turned(): pl.pallas_call(functools.partial(range_kernel, talk=talk), out_shape=jax....  112 us
    pallas_call x1, Pallas kernels, focused(): pl.pallas_call(functools.partial(azimuth_kernel, split=split), out_shape=...  35.8 us
    pallas_call x1, Pallas kernels, own_map(): pl.pallas_call(map_kernel, out_shape=jax.ShapeDtypeStruct((2, R2), F32),...  18.5 us

profile of v1, /device:TPU:1, one launch (start us, length us, event | category | flops | bytes accessed | tf_op | source)
XLA Modules:
  0.0 169.7 jit_solution(15019815112273284210)
XLA Ops:
  0.6 1.6 reshape.19.phase
  2.2 112.0 %range_lines.1 = bf16[4,256,16,128]{3,2,1,0:T(8,128)(2,1)} custom-call(bf16[2,32,32768]{2,1,0:T(8,128)(2,1)} %x_hbm.1, f32[32]{0:T(128)} %rate.1, f32[32]{0:T(128)} %shift.1, f32[128,256]{1,0:T(8,128)} %reshape.19.phase, bf16[512,512]{1,0:T(8,128)(2,1)} %constant.26.clone.args_0_, bf16[256,256]{1,0:T(8,128)(2,1)} %constant.27.clone.args_1_, ...), custom_call_target="tpu_custom_call" | custom-call | flops 7000000000 | bytes 10000000 | tf_op jit(solution)/shard_map/range_lines/pallas_call | solution.py:299
  114.2 35.8 %azimuth_columns.1 = (bf16[2,16,16,32,128]{4,3,2,1,0:T(8,128)(2,1)}, f32[32,512]{1,0:T(8,128)}) custom-call(bf16[4,16,16,16,128]{4,3,2,1,0:T(8,128)(2,1)} %bitcast.9, bf16[16,256,256]{2,1,0:T(8,128)(2,1)} %constant.33.clone.t1, bf16[4,256,256]{2,1,0:T(8,128)(2,1)} %constant.34.clone.t2, bf16[16,256,256]{2,1,0:T(8,128)(2,1)} %constant.35.clone.t3, ...), custom_call_target="tpu_custom_call" | custom-call | flops 15000000512 | bytes 20000000 | tf_op jit(solution)/shard_map/azimuth_columns/pallas_call | solution.py:495
  150.0 18.5 %phase_rows.1 = f32[2,128]{1,0:T(2,128)} custom-call(f32[32,512]{1,0:T(8,128)} %get-tuple-element.5.terms, s32[1,32]{1,0:T(1,128)} %bitcast.6), custom_call_target="tpu_custom_call" | custom-call | tf_op jit(solution)/shard_map/phase_rows/pallas_call | solution.py:609
  168.5 1.2 copy.24

commit v2 on v1

--- a/solution.py
+++ b/solution.py
@@ -95,12 +95,40 @@
     return jnp.dot(a, b, preferred_element_type=F32)
 
 
+def pair(one, other):
+    return jnp.concatenate([one.reshape(256, R2), other.reshape(256, R2)], axis=1)
+
+
+def halves(out):
+    out = out.astype(BF16)
+    return [out[:, R2 * i : R2 * i + R2].reshape(16, 16, R2) for i in range(2)]
+
+
+def first_stages(h, r, y, z, first, second):
+    def one(s, _):
+        out = halves(dot(first[s], pair(r[2 * h, :, s], r[2 * h + 1, :, s])))
+        for i in range(2):
+            y[2 * h + i, :, s] = out[i]
+        return 0
+
+    lax.fori_loop(0, 16, one, 0, unroll=4)
+    for c in (2 * h, 2 * h + 1):
+
+        def two(k, _):
+            out = halves(dot(second[c], pair(y[c, 2 * k], y[c, 2 * k + 1])))
+            for i in range(2):
+                z[:, 2 * k + i, c] = out[i]
+            return 0
+
+        lax.fori_loop(0, 8, two, 0, unroll=4)
+
+
 def range_kernel(
     x_hbm, rate, shift, phase, *args, talk=True,
 ):
-    sources, out_hbm, tables = args[:7], args[7], args[8:15]
-    raw, xbuf, rp, rows, send, in_sem, tab_sem, send_sem, recv_sem, own_sem = args[15:]
-    first, inner, outer, last, swap, cross, planes = tables
+    sources, out_hbm, tables = args[:9], args[9], args[10:19]
+    raw, xbuf, rp, rows, send, got, y, z, in_sem, tab_sem, send_sem, recv_sem, own_sem, out_sem = args[19:]
+    first, inner, outer, last, swap, cross, planes, az_first, az_second = tables
     loads = [
         pltpu.make_async_copy(x_hbm.at[:, pl.ds(16 * h, 16)], raw.at[h], in_sem.at[h]) for h in range(2)
     ]
@@ -109,12 +137,16 @@
     for i in (5, 6, 0, 1, 2, 3, 4):
         copies[i].start()
     loads[1].start()
-    rp[...] = phase[...].T * (1.0 / TWO_PI)
+    copies[7].start()
+    copies[8].start()
+    for i in range(2):
+        rp[R2 * i : R2 * i + R2] = phase[pl.ds(i, R2, stride=2), :].T * (1.0 / TWO_PI)
     copies[5].wait()
     if talk:
         form = lax.axis_index("form")
         focus = lax.axis_index("focus")
         me = form * 4 + focus
+        me_hi, me_lo = lax.div(me, 16), lax.rem(me, 16)
         barrier = pltpu.get_barrier_semaphore()
 
         def greet(j, _):
@@ -249,7 +281,7 @@
         def _():
             pl.semaphore_wait(barrier, 255)
 
-        pltpu.make_async_copy(send.at[c, me], out_hbm.at[c, me], own_sem).start()
+        pltpu.make_async_copy(send.at[c, me], got.at[c, me_hi, me_lo], own_sem.at[c]).start()
 
         def sends(j, _):
             dy = lax.rem(j, 4)
@@ -263,9 +295,9 @@
                 def go():
                     pltpu.make_async_remote_copy(
                         src_ref=send.at[c, group * 4 + other],
-                        dst_ref=out_hbm.at[c, me],
+                        dst_ref=got.at[c, me_hi, me_lo],
                         send_sem=send_sem,
-                        recv_sem=recv_sem,
+                        recv_sem=recv_sem.at[c],
                         device_id=(group, other),
                         device_id_type=MESH,
                     ).start()
@@ -280,26 +312,38 @@
         return 0
 
     lax.fori_loop(0, CHUNKS, chunk, 0)
-    if not talk:
-        copy = pltpu.make_async_copy(send, out_hbm, own_sem)
-        copy.start()
-        copy.wait()
-        return
-    pltpu.make_async_copy(send.at[:, 0], out_hbm.at[:, 0], own_sem).wait()
-    pltpu.make_async_copy(send.at[:, pl.ds(0, 255)], out_hbm.at[:, pl.ds(0, 255)], send_sem).wait()
-    pltpu.make_async_copy(send.at[:, pl.ds(0, 255)], out_hbm.at[:, pl.ds(0, 255)], recv_sem).wait()
+    for h in range(2):
+        if h == 0:
+            copies[7].wait()
+            copies[8].wait()
+        if talk:
+            for c in (2 * h, 2 * h + 1):
+                pltpu.make_async_copy(send.at[c, 0], got.at[c, 0, 0], own_sem.at[c]).wait()
+                pltpu.make_async_copy(
+                    send.at[c, pl.ds(0, 255)], send.at[c, pl.ds(0, 255)], recv_sem.at[c]
+                ).wait()
+        first_stages(h, got, y, z, az_first, az_second)
+        pltpu.make_async_copy(
+            z.at[:, :, pl.ds(2 * h, 2)], out_hbm.at[:, :, pl.ds(2 * h, 2)], out_sem.at[h]
+        ).start()
+    if talk:
+        pltpu.make_async_copy(send.at[:, pl.ds(0, 255)], send.at[:, pl.ds(0, 255)], send_sem).wait()
+    for h in range(2):
+        pltpu.make_async_copy(
+            z.at[:, :, pl.ds(2 * h, 2)], out_hbm.at[:, :, pl.ds(2 * h, 2)], out_sem.at[h]
+        ).wait()
 
 
 def corner_turned(echoes, rate, shift, range_phase, talk=True):
-    phase = range_phase.reshape(R2, R1)
-    tables = range_tables()
+    phase = range_phase.reshape(R1, R2)
+    tables = range_tables() + azimuth_tables()[:2]
     vmem = pl.BlockSpec(memory_space=pltpu.VMEM)
     smem = pl.BlockSpec(memory_space=pltpu.SMEM)
     hbm = pl.BlockSpec(memory_space=pl.ANY)
     return pl.pallas_call(
         functools.partial(range_kernel, talk=talk),
-        out_shape=jax.ShapeDtypeStruct((CHUNKS, 256, 2 * LINES, R2), BF16),
-        in_specs=[hbm, smem, smem, vmem] + [hbm] * 7,
+        out_shape=jax.ShapeDtypeStruct((16, 16, CHUNKS, 16, R2), BF16),
+        in_specs=[hbm, smem, smem, vmem] + [hbm] * 9,
         out_specs=hbm,
         scratch_shapes=[
             *[pltpu.VMEM(t.shape, t.dtype) for t in tables],
@@ -308,11 +352,15 @@
             pltpu.VMEM((R1, R2), F32),
             pltpu.VMEM((LINES, 2, R1, R2), BF16),
             pltpu.VMEM((CHUNKS, 256, 2 * LINES, R2), BF16),
+            pltpu.VMEM((CHUNKS, 16, 16, 16, R2), BF16),
+            pltpu.VMEM((CHUNKS, 16, 16, 16, R2), BF16),
+            pltpu.VMEM((16, 16, CHUNKS, 16, R2), BF16),
             pltpu.SemaphoreType.DMA((2,)),
-            pltpu.SemaphoreType.DMA((7,)),
+            pltpu.SemaphoreType.DMA((9,)),
             pltpu.SemaphoreType.DMA,
-            pltpu.SemaphoreType.DMA,
-            pltpu.SemaphoreType.DMA,
+            pltpu.SemaphoreType.DMA((CHUNKS,)),
+            pltpu.SemaphoreType.DMA((CHUNKS,)),
+            pltpu.SemaphoreType.DMA((2,)),
         ],
         compiler_params=pltpu.CompilerParams(
             has_side_effects=True, vmem_limit_bytes=62 * 2**20, **({"collective_id": 0} if talk else {})
@@ -323,25 +371,23 @@
 
 
 def azimuth_kernel(
-    r_hbm, t1, t2, t3, t4, t5, t6, rate, listed, held, img_hbm, terms,
+    z_hbm, t1, t2, t3, t4, t5, t6, rate, listed, held, img_hbm, terms,
     r, y, z, back, v, first, second, third, fourth, fifth, sixth, img, sums, sel, centers, sems, tab_sems, out_sem, *, split=True,
 ):
-    loads = [
-        pltpu.make_async_copy(r_hbm.at[pl.ds(2 * h, 2)], r.at[pl.ds(2 * h, 2)], sems.at[h])
-        for h in range(2)
-    ]
+    def batch(g):
+        part = pl.ds(4 * g, 4)
+        refs = [(z_hbm.at[:, part], z.at[:, part]), (t3.at[part], third.at[part]), (t4.at[part], fourth.at[part])]
+        return [pltpu.make_async_copy(a, b, sems.at[g, i]) for i, (a, b) in enumerate(refs)]
+
+    for g in range(4):
+        for copy in batch(g):
+            copy.start()
     tables = [
         pltpu.make_async_copy(a, b, tab_sems.at[i])
-        for i, (a, b) in enumerate(
-            [(t1, first), (t2, second), (t3, third), (t4, fourth), (t5, fifth), (t6, sixth)]
-        )
+        for i, (a, b) in enumerate([(t5, fifth), (t6, sixth), (t1, first), (t2, second)])
     ]
-    tables[0].start()
-    loads[0].start()
-    loads[1].start()
-    for i in range(1, 6):
-        tables[i].start()
-
+    for copy in tables:
+        copy.start()
     own = lax.axis_index("focus") * R2 if split else 0
     centers[...] = jnp.zeros((2, R2), jnp.int32) - 1
     centers[0:1, :LISTED] = held[...]
@@ -349,45 +395,9 @@
     column = lax.broadcasted_iota(jnp.int32, (R2, R2), 0)
     sel[...] = jnp.where(column == centers[1:2], 1.0, 0.0).astype(BF16)
 
-    def pair(one, other):
-        return jnp.concatenate([one.reshape(256, R2), other.reshape(256, R2)], axis=1)
-
-    def halves(out):
-        out = out.astype(BF16)
-        return [out[:, R2 * i : R2 * i + R2].reshape(16, 16, R2) for i in range(2)]
-
-    def forward(wait):
-        for h in range(2):
-            if wait:
-                if h == 0:
-                    tables[0].wait()
-                loads[h].wait()
-
-            def one(s, _):
-                out = halves(dot(first[s], pair(r[2 * h, :, s], r[2 * h + 1, :, s])))
-                for i in range(2):
-                    y[2 * h + i, :, s] = out[i]
-                return 0
-
-            lax.fori_loop(0, 16, one, 0, unroll=4)
-        if wait:
-            tables[1].wait()
-        for c in range(CHUNKS):
-
-            def two(k, _):
-                out = halves(dot(second[c], pair(y[c, 2 * k], y[c, 2 * k + 1])))
-                for i in range(2):
-                    z[:, 2 * k + i, c] = out[i]
-                return 0
-
-            lax.fori_loop(0, 8, two, 0, unroll=4)
-
     def spectrum(k, h):
         return dot(third[k], pair(z[pl.ds(8 * h, 4), k], z[pl.ds(8 * h + 4, 4), k]))
 
-    forward(True)
-    for i in range(2, 6):
-        tables[i].wait()
     m = lax.broadcasted_iota(jnp.int32, (32, R2), 0)
     m = jnp.where(m >= 16, m - 32, m).astype(F32) * (1.0 / 32)
     cycles = rate[...] * (1.0 / TWO_PI)
@@ -411,7 +421,12 @@
             back[pl.ds(8 * h + 4 * i, 4), k] = out[:, R2 * i : R2 * i + R2].reshape(4, 4, 16, R2)
         return 0
 
-    lax.fori_loop(0, 32, filtered, 0, unroll=2)
+    for g in range(4):
+        for copy in batch(g):
+            copy.wait()
+        lax.fori_loop(8 * g, 8 * g + 8, filtered, 0, unroll=2)
+    tables[0].wait()
+    tables[1].wait()
     for c in range(CHUNKS):
 
         def three(k, _):
@@ -452,7 +467,10 @@
         return 0
 
     lax.fori_loop(0, 32, windowed, 0, unroll=2)
-    forward(False)
+    tables[2].wait()
+    tables[3].wait()
+    for h in range(2):
+        first_stages(h, r, y, z, first, second)
 
     def line_spectrum(j, _):
         k, h = lax.div(j, 2), lax.rem(j, 2)
@@ -484,7 +502,7 @@
         return 0
 
     lax.fori_loop(0, 8, group, 0)
-    terms[...] = sums[...].T[:LISTED]
+    terms[...] = sums[...].T[:LISTED].astype(BF16)
     image_out.wait()
 
 
@@ -496,7 +514,7 @@
         functools.partial(azimuth_kernel, split=split),
         out_shape=(
             jax.ShapeDtypeStruct((2, 16, 16, 32, R2), BF16),
-            jax.ShapeDtypeStruct((LISTED, 512), F32),
+            jax.ShapeDtypeStruct((LISTED, 512), BF16),
         ),
         in_specs=[hbm] * 7 + [vmem] * 3,
         out_specs=(hbm, vmem),
@@ -511,114 +529,89 @@
             pltpu.VMEM((512, R2), F32),
             pltpu.VMEM((R2, R2), BF16),
             pltpu.VMEM((2, R2), jnp.int32),
-            pltpu.SemaphoreType.DMA((2,)),
-            pltpu.SemaphoreType.DMA((6,)),
+            pltpu.SemaphoreType.DMA((4, 3)),
+            pltpu.SemaphoreType.DMA((4,)),
             pltpu.SemaphoreType.DMA,
         ],
         compiler_params=pltpu.CompilerParams(vmem_limit_bytes=62 * 2**20),
         cost_estimate=pl.CostEstimate(flops=15 * 10**9, bytes_accessed=2 * 10**7, transcendentals=0),
         name="azimuth_columns",
-    )(arrived.reshape(4, 16, 16, 16, R2), *[jnp.asarray(t) for t in tables], rate[None], listed, held)
+    )(arrived, *[jnp.asarray(t) for t in tables], rate[None], listed, held)
     return image.reshape(2, AZ, R2), terms
 
 
-def map_kernel(terms, blocks, out, got, rows, parts, send_sem, recv_sem, row_send, row_recv):
+def map_kernel(terms, blocks, out, got, rows, parts, sums, ends, sems):
     form = lax.axis_index("form")
     focus = lax.axis_index("focus")
+    row, ring = lax.rem(form, 8), lax.div(form, 8)
+
+    def wrapped(value, size):
+        return jnp.where(value >= size, value - size, value)
+
+    mates = [(form, wrapped(focus + d, 4)) for d in range(1, 4)]
+    across = [wrapped(row + d, 8) for d in range(1, 8)]
+    along = [wrapped(ring + d, 8) for d in range(1, 8)]
     barrier = pltpu.get_barrier_semaphore()
-    for d in range(1, 4):
-        other = focus + d
-        other = jnp.where(other >= 4, other - 4, other)
-        pl.semaphore_signal(barrier, inc=1, device_id=(form, other), device_id_type=MESH)
-
-    def greet(j, _):
-        for dz in range(8):
-            other = form + j + 8 * dz
-            other = jnp.where(other >= 64, other - 64, other)
-
-            def hello():
-                pl.semaphore_signal(barrier, inc=1, device_id=(other, focus), device_id_type=MESH)
-
-            if dz == 0:
-                pl.when(j > 0)(hello)
-            else:
-                hello()
-        return 0
-
-    lax.fori_loop(0, 8, greet, 0)
-    own = 4 * lax.broadcasted_iota(jnp.int32, (64, LISTED), 0) + focus
-    chosen = jnp.where(own == blocks[...], 1.0, 0.0)
-    pl.semaphore_wait(barrier, 66)
-    copies = []
-    for d in range(1, 4):
-        other = focus + d
-        other = jnp.where(other >= 4, other - 4, other)
-        copies.append(
-            pltpu.make_async_remote_copy(
-                src_ref=terms,
-                dst_ref=got.at[d - 1],
-                send_sem=send_sem.at[d - 1],
-                recv_sem=recv_sem.at[d - 1],
-                device_id=(form, other),
-                device_id_type=MESH,
-            )
+    for peer in mates + [(ring * 8 + r, focus) for r in across] + [(z * 8 + row, focus) for z in along]:
+        pl.semaphore_signal(barrier, inc=1, device_id=peer, device_id_type=MESH)
+    place = lax.broadcasted_iota(jnp.int32, (64, LISTED), 0)
+    own = (jnp.bitwise_and(place, 7) * 8 + jnp.right_shift(place, 3)) * 4 + focus
+    chosen = jnp.where(own == blocks[...], 1.0, 0.0).astype(BF16)
+    pl.semaphore_wait(barrier, 17)
+
+    def send(src, dst, i, peer):
+        copy = pltpu.make_async_remote_copy(
+            src_ref=src,
+            dst_ref=dst,
+            send_sem=sems.at[2 * i],
+            recv_sem=sems.at[2 * i + 1],
+            device_id=peer,
+            device_id_type=MESH,
         )
-        copies[-1].start()
-    for copy in copies:
+        copy.start()
+        return copy
+
+    started = [send(terms, got.at[d], d, mates[d]) for d in range(3)]
+    for copy in started:
         copy.wait_recv()
-    group = terms[...] + got[0] + (got[1] + got[2])
-    mine = jnp.dot(
-        chosen, group, preferred_element_type=F32, precision=lax.Precision.HIGHEST
-    )
+    group = terms[...].astype(F32) + got[0].astype(F32) + (got[1].astype(F32) + got[2].astype(F32))
+    mine = dot(chosen, group.astype(BF16))
     for i in range(4):
         rows[:, i] = mine[:, R2 * i : R2 * i + R2]
-    parts[form] = rows[form]
-
-    def sends(j, _):
-        for dz in (4, 3, 5, 2, 6, 1, 7, 0):
-            other = form + j + 8 * dz
-            other = jnp.where(other >= 64, other - 64, other)
-
-            def go():
-                pltpu.make_async_remote_copy(
-                    src_ref=rows.at[other],
-                    dst_ref=parts.at[form],
-                    send_sem=row_send,
-                    recv_sem=row_recv,
-                    device_id=(other, focus),
-                    device_id_type=MESH,
-                ).start()
-
-            if dz == 0:
-                pl.when(j > 0)(go)
-            else:
-                go()
-        return 0
-
-    lax.fori_loop(0, 8, sends, 0)
-    for copy in copies:
+    second = [
+        send(rows.at[pl.ds(8 * r, 8)], parts.at[d], 3 + d, (ring * 8 + r, focus))
+        for d, r in enumerate(across)
+    ]
+    total = rows[pl.ds(8 * row, 8)]
+    for d, copy in enumerate(second):
+        copy.wait_recv()
+        total += parts[d]
+    sums[...] = total
+    third = [send(sums.at[z], ends.at[d], 10 + d, (z * 8 + row, focus)) for d, z in enumerate(along)]
+    total = sums[ring]
+    for d, copy in enumerate(third):
+        copy.wait_recv()
+        total += ends[d]
+    for i in range(2):
+        out[:, R2 * i : R2 * i + R2] = total[i : i + 1] / (total[2 + i : 3 + i] + EPSILON)
+    for copy in started + second + third:
         copy.wait_send()
-    pltpu.make_async_copy(rows.at[pl.ds(0, 63)], parts.at[pl.ds(0, 63)], row_send).wait()
-    pltpu.make_async_copy(rows.at[pl.ds(0, 63)], parts.at[pl.ds(0, 63)], row_recv).wait()
-    total = jnp.sum(parts[...], axis=0)
-    out[...] = total[:2] / (total[2:] + EPSILON)
 
 
 def own_map(terms, blocks):
     vmem = pl.BlockSpec(memory_space=pltpu.VMEM)
     return pl.pallas_call(
         map_kernel,
-        out_shape=jax.ShapeDtypeStruct((2, R2), F32),
+        out_shape=jax.ShapeDtypeStruct((1, 2 * R2), F32),
         in_specs=[vmem, vmem],
         out_specs=vmem,
         scratch_shapes=[
-            pltpu.VMEM((3, LISTED, 512), F32),
+            pltpu.VMEM((3, LISTED, 512), BF16),
             pltpu.VMEM((64, 4, R2), F32),
-            pltpu.VMEM((64, 4, R2), F32),
-            pltpu.SemaphoreType.DMA((3,)),
-            pltpu.SemaphoreType.DMA((3,)),
-            pltpu.SemaphoreType.DMA,
-            pltpu.SemaphoreType.DMA,
+            pltpu.VMEM((7, 8, 4, R2), F32),
+            pltpu.VMEM((8, 4, R2), F32),
+            pltpu.VMEM((7, 4, R2), F32),
+            pltpu.SemaphoreType.DMA((34,)),
         ],
         compiler_params=pltpu.CompilerParams(
             has_side_effects=True, vmem_limit_bytes=62 * 2**20, collective_id=1
@@ -639,7 +632,7 @@
 ):
     arrived = corner_turned(echoes, scale_rate, migration, range_phase)
     focused_image, terms = focused(arrived, azimuth_rate, bright_columns, line_center)
-    phase_map = own_map(terms, line_block.reshape(1, LISTED)).reshape(1, 256)
+    phase_map = own_map(terms, line_block.reshape(1, LISTED))
     return (focused_image, phase_map)
 
 

time: 170 us -> 163 us (0.959)
  Pallas kernels: 166 us -> 161 us
    pallas_call x1, Pallas kernels: 35.8 us -> 28.9 us  [focused(): pl.pallas_call(functools.partial(azimuth_kernel, split=split), out_shape=...]
    pallas_call x1, Pallas kernels: 112 us -> 116 us  [corner_turned(): pl.pallas_call(functools.partial(range_kernel, talk=talk), out_shape=jax....]
    pallas_call x1, Pallas kernels: 18.5 us -> 16.5 us  [own_map(): pl.pallas_call(map_kernel, out_shape=jax.ShapeDtypeStruct((1, 2 * R2), F3...]
where the time goes in v2:
time: 163 us
  Pallas kernels  161 us (99%)
    pallas_call x1, Pallas kernels, corner_turned(): pl.pallas_call(functools.partial(range_kernel, talk=talk), out_shape=jax....  116 us
    pallas_call x1, Pallas kernels, focused(): pl.pallas_call(functools.partial(azimuth_kernel, split=split), out_shape=...  28.9 us
    pallas_call x1, Pallas kernels, own_map(): pl.pallas_call(map_kernel, out_shape=jax.ShapeDtypeStruct((1, 2 * R2), F3...  16.5 us

profile of v2, /device:TPU:1, one launch (start us, length us, event | category | flops | bytes accessed | tf_op | source)
XLA Modules:
  0.0 163.1 jit_solution(3462329219827457811)
XLA Ops:
  0.6 115.9 %range_lines.1.z_hbm = bf16[16,16,4,16,128]{4,3,2,1,0:T(8,128)(2,1)} custom-call(bf16[2,32,32768]{2,1,0:T(8,128)(2,1)} %x_hbm.1, f32[32]{0:T(128)} %rate.1, f32[32]{0:T(128)} %shift.1, f32[256,128]{1,0:T(8,128)} %bitcast.5, bf16[512,512]{1,0:T(8,128)(2,1)} %constant.26.clone.args_0_, bf16[256,256]{1,0:T(8,128)(2,1)} %constant.27.clone.args_1_, ...), custom_call_target="tpu_custom_call" | custom-call | flops 7000000000 | bytes 10000000 | tf_op jit(solution)/shard_map/range_lines/pallas_call | solution.py:343
  116.5 28.9 %azimuth_columns.1 = (bf16[2,16,16,32,128]{4,3,2,1,0:T(8,128)(2,1)}, bf16[32,512]{1,0:T(8,128)(2,1)}) custom-call(bf16[16,16,4,16,128]{4,3,2,1,0:T(8,128)(2,1)} %range_lines.1.z_hbm, bf16[16,256,256]{2,1,0:T(8,128)(2,1)} %constant.33.clone.args_7_.t1, bf16[4,256,256]{2,1,0:T(8,128)(2,1)} %constant.34.clone.args_8_.t2, ...), custom_call_target="tpu_custom_call" | custom-call | flops 15000000512 | bytes 20000000 | tf_op jit(solution)/shard_map/azimuth_columns/pallas_call | solution.py:513
  145.4 16.5 %phase_rows.1 = f32[1,256]{1,0:T(1,128)} custom-call(bf16[32,512]{1,0:T(8,128)(2,1)} %get-tuple-element.5.terms, s32[1,32]{1,0:T(1,128)} %bitcast.4), custom_call_target="tpu_custom_call" | custom-call | tf_op jit(solution)/shard_map/phase_rows/pallas_call | solution.py:603
  161.9 1.2 copy.26

commit v3 on v2

--- a/solution.py
+++ b/solution.py
@@ -111,7 +111,7 @@
             y[2 * h + i, :, s] = out[i]
         return 0
 
-    lax.fori_loop(0, 16, one, 0, unroll=4)
+    lax.fori_loop(0, 16, one, 0, unroll=8)
     for c in (2 * h, 2 * h + 1):
 
         def two(k, _):
@@ -120,7 +120,11 @@
                 z[:, 2 * k + i, c] = out[i]
             return 0
 
-        lax.fori_loop(0, 8, two, 0, unroll=4)
+        lax.fori_loop(0, 8, two, 0, unroll=8)
+
+
+def spectrum(z, third, k, h):
+    return dot(third[k], pair(z[pl.ds(8 * h, 4), k], z[pl.ds(8 * h + 4, 4), k]))
 
 
 def range_kernel(
@@ -134,7 +138,36 @@
     ]
     copies = [pltpu.make_async_copy(a, b, tab_sem.at[i]) for i, (a, b) in enumerate(zip(sources, tables))]
     loads[0].start()
-    for i in (5, 6, 0, 1, 2, 3, 4):
+    copies[5].start()
+    if talk:
+        form = lax.axis_index("form")
+        focus = lax.axis_index("focus")
+        me = form * 4 + focus
+        me_hi, me_lo = lax.div(me, 16), lax.rem(me, 16)
+        barrier = pltpu.get_barrier_semaphore()
+
+        others = [focus] + [jnp.where(focus >= 4 - dy, focus + dy - 4, focus + dy) for dy in range(1, 4)]
+
+        def greet(j, _):
+            for d in range(8):
+                group = form + j + 8 * d
+                group = jnp.where(group >= 64, group - 64, group)
+                for dy in range(4):
+
+                    def hello():
+                        pl.semaphore_signal(
+                            barrier, inc=1, device_id=(group, others[dy]), device_id_type=MESH
+                        )
+
+                    if d == 0 and dy == 0:
+                        pl.when(j > 0)(hello)
+                    else:
+                        hello()
+            return 0
+
+        lax.fori_loop(0, 8, greet, 0)
+
+    for i in (6, 0, 1, 2, 3, 4):
         copies[i].start()
     loads[1].start()
     copies[7].start()
@@ -142,34 +175,6 @@
     for i in range(2):
         rp[R2 * i : R2 * i + R2] = phase[pl.ds(i, R2, stride=2), :].T * (1.0 / TWO_PI)
     copies[5].wait()
-    if talk:
-        form = lax.axis_index("form")
-        focus = lax.axis_index("focus")
-        me = form * 4 + focus
-        me_hi, me_lo = lax.div(me, 16), lax.rem(me, 16)
-        barrier = pltpu.get_barrier_semaphore()
-
-        def greet(j, _):
-            for d in range(8):
-                group = form + j + 8 * d
-                group = jnp.where(group >= 64, group - 64, group)
-                for dy in range(4):
-                    other = focus + dy
-                    other = jnp.where(other >= 4, other - 4, other)
-
-                    def hello():
-                        pl.semaphore_signal(
-                            barrier, inc=1, device_id=(group, other), device_id_type=MESH
-                        )
-
-                    if d == 0 and dy == 0:
-                        pl.when(j > 0)(hello)
-                    else:
-                        hello()
-            return 0
-
-        lax.fori_loop(0, 8, greet, 0)
-
     def chunk(c, _):
         h = lax.div(c, 2)
 
@@ -371,8 +376,7 @@
 
 
 def azimuth_kernel(
-    z_hbm, t1, t2, t3, t4, t5, t6, rate, listed, held, img_hbm, terms,
-    r, y, z, back, v, first, second, third, fourth, fifth, sixth, img, sums, sel, centers, sems, tab_sems, out_sem, *, split=True,
+    z_hbm, t3, t4, t5, t6, rate, img_hbm, y, z, back, third, fourth, fifth, sixth, img, sems, tab_sems, out_sem,
 ):
     def batch(g):
         part = pl.ds(4 * g, 4)
@@ -384,27 +388,17 @@
             copy.start()
     tables = [
         pltpu.make_async_copy(a, b, tab_sems.at[i])
-        for i, (a, b) in enumerate([(t5, fifth), (t6, sixth), (t1, first), (t2, second)])
+        for i, (a, b) in enumerate([(t5, fifth), (t6, sixth)])
     ]
     for copy in tables:
         copy.start()
-    own = lax.axis_index("focus") * R2 if split else 0
-    centers[...] = jnp.zeros((2, R2), jnp.int32) - 1
-    centers[0:1, :LISTED] = held[...]
-    centers[1:2, :LISTED] = listed[...] - own
-    column = lax.broadcasted_iota(jnp.int32, (R2, R2), 0)
-    sel[...] = jnp.where(column == centers[1:2], 1.0, 0.0).astype(BF16)
-
-    def spectrum(k, h):
-        return dot(third[k], pair(z[pl.ds(8 * h, 4), k], z[pl.ds(8 * h + 4, 4), k]))
-
     m = lax.broadcasted_iota(jnp.int32, (32, R2), 0)
     m = jnp.where(m >= 16, m - 32, m).astype(F32) * (1.0 / 32)
     cycles = rate[...] * (1.0 / TWO_PI)
 
     def filtered(j, _):
         k, h = lax.div(j, 2), lax.rem(j, 2)
-        out = spectrum(k, h)
+        out = spectrum(z, third, k, h)
         columns = []
         for i in range(2):
             rows = []
@@ -424,7 +418,7 @@
     for g in range(4):
         for copy in batch(g):
             copy.wait()
-        lax.fori_loop(8 * g, 8 * g + 8, filtered, 0, unroll=2)
+        lax.fori_loop(8 * g, 8 * g + 8, filtered, 0, unroll=8)
     tables[0].wait()
     tables[1].wait()
     for c in range(CHUNKS):
@@ -435,7 +429,7 @@
                 y[c, :, 2 * k + i] = out[i]
             return 0
 
-        lax.fori_loop(0, 8, three, 0, unroll=4)
+        lax.fori_loop(0, 8, three, 0, unroll=8)
     for h in range(2):
 
         def four(s, _):
@@ -446,9 +440,79 @@
                 img[a, :, s, 16 * h : 16 * h + 16] = out[:, a]
             return 0
 
-        lax.fori_loop(0, 16, four, 0, unroll=4)
-    image_out = pltpu.make_async_copy(img, img_hbm, out_sem)
-    image_out.start()
+        if h == 0:
+            lax.fori_loop(0, 16, four, 0, unroll=8)
+    leaving = []
+    for g in range(2):
+        lax.fori_loop(8 * g, 8 * g + 8, four, 0, unroll=8)
+        part = pl.ds(8 * g, 8)
+        leaving.append(pltpu.make_async_copy(img.at[:, :, part], img_hbm.at[:, :, part], out_sem.at[g]))
+        leaving[-1].start()
+    for copy in leaving:
+        copy.wait()
+
+
+def focused(arrived, rate):
+    vmem = pl.BlockSpec(memory_space=pltpu.VMEM)
+    hbm = pl.BlockSpec(memory_space=pl.ANY)
+    tables = azimuth_tables()[2:]
+    return pl.pallas_call(
+        azimuth_kernel,
+        out_shape=jax.ShapeDtypeStruct((2, 16, 16, 32, R2), BF16),
+        in_specs=[hbm] * 5 + [vmem],
+        out_specs=hbm,
+        scratch_shapes=[
+            pltpu.VMEM((4, 16, 16, 16, R2), BF16),
+            pltpu.VMEM((16, 16, 4, 16, R2), BF16),
+            pltpu.VMEM((16, 16, 4, 16, R2), BF16),
+            *[pltpu.VMEM(t.shape, BF16) for t in tables],
+            pltpu.VMEM((2, 16, 16, 32, R2), BF16),
+            pltpu.SemaphoreType.DMA((4, 3)),
+            pltpu.SemaphoreType.DMA((2,)),
+            pltpu.SemaphoreType.DMA((2,)),
+        ],
+        compiler_params=pltpu.CompilerParams(vmem_limit_bytes=62 * 2**20),
+        cost_estimate=pl.CostEstimate(flops=15 * 10**9, bytes_accessed=2 * 10**7, transcendentals=0),
+        name="azimuth_columns",
+    )(arrived, *[jnp.asarray(t) for t in tables], rate[None])
+
+
+def lines_kernel(
+    img_hbm, t1, t2, t3, listed, held, blocks, out, img, r, y, z, v, first, second, third, table, sel, centers, terms,
+    got, rows, parts, sums, ends, img_sems, tab_sems, sems,
+):
+    pieces = [
+        pltpu.make_async_copy(img_hbm.at[:, pl.ds(4 * g, 4)], img.at[:, pl.ds(4 * g, 4)], img_sems.at[g])
+        for g in range(4)
+    ]
+    tables = [
+        pltpu.make_async_copy(a, b, tab_sems.at[i])
+        for i, (a, b) in enumerate([(t1, first), (t2, second), (t3, third)])
+    ]
+    for copy in pieces + tables:
+        copy.start()
+    form = lax.axis_index("form")
+    focus = lax.axis_index("focus")
+    row, ring = lax.rem(form, 8), lax.div(form, 8)
+
+    def wrapped(value, size):
+        return jnp.where(value >= size, value - size, value)
+
+    mates = [(form, wrapped(focus + d, 4)) for d in range(1, 4)]
+    across = [wrapped(row + d, 8) for d in range(1, 8)]
+    along = [wrapped(ring + d, 8) for d in range(1, 8)]
+    barrier = pltpu.get_barrier_semaphore()
+    for peer in mates + [(ring * 8 + r, focus) for r in across] + [(z * 8 + row, focus) for z in along]:
+        pl.semaphore_signal(barrier, inc=1, device_id=peer, device_id_type=MESH)
+    place = lax.broadcasted_iota(jnp.int32, (64, LISTED), 0)
+    own = (jnp.bitwise_and(place, 7) * 8 + jnp.right_shift(place, 3)) * 4 + focus
+    chosen = jnp.where(own == blocks[...], 1.0, 0.0).astype(BF16)
+    own = focus * R2
+    centers[...] = jnp.zeros((2, R2), jnp.int32) - 1
+    centers[0:1, :LISTED] = held[...]
+    centers[1:2, :LISTED] = listed[...] - own
+    column = lax.broadcasted_iota(jnp.int32, (R2, R2), 0)
+    sel[...] = jnp.where(column == centers[1:2], 1.0, 0.0).astype(BF16)
 
     line = lax.broadcasted_iota(jnp.int32, (256, R2), 0)
 
@@ -466,20 +530,22 @@
             r[c, hi, pl.ds(lo, 8)] = both[:, c].reshape(8, 16, R2)
         return 0
 
-    lax.fori_loop(0, 32, windowed, 0, unroll=2)
-    tables[2].wait()
-    tables[3].wait()
+    for g in range(4):
+        pieces[g].wait()
+        lax.fori_loop(8 * g, 8 * g + 8, windowed, 0, unroll=4)
+    for copy in tables:
+        copy.wait()
     for h in range(2):
         first_stages(h, r, y, z, first, second)
 
     def line_spectrum(j, _):
         k, h = lax.div(j, 2), lax.rem(j, 2)
-        out = spectrum(k, h)
+        out = spectrum(z, third, k, h)
         for i in range(2):
             v[pl.ds(8 * h + 4 * i, 4), k] = out[:, R2 * i : R2 * i + R2].reshape(4, 2, 32, R2)
         return 0
 
-    lax.fori_loop(0, 32, line_spectrum, 0, unroll=4)
+    lax.fori_loop(0, 32, line_spectrum, 0, unroll=8)
     end_re, end_im = pltpu.roll(v[0, 0, 0], 31, 0), pltpu.roll(v[0, 0, 1], 31, 0)
 
     def group(g, _):
@@ -497,66 +563,12 @@
             cross += re * next_im - im * next_re
             energy += re * re + im * im
             re, im = next_re, next_im
-        sums[pl.ds(g, 32, stride=8)] = cross
-        sums[pl.ds(256 + g, 32, stride=8)] = energy
+        table[pl.ds(g, 32, stride=8)] = cross
+        table[pl.ds(256 + g, 32, stride=8)] = energy
         return 0
 
     lax.fori_loop(0, 8, group, 0)
-    terms[...] = sums[...].T[:LISTED].astype(BF16)
-    image_out.wait()
-
-
-def focused(arrived, rate, listed, held, split=True):
-    vmem = pl.BlockSpec(memory_space=pltpu.VMEM)
-    hbm = pl.BlockSpec(memory_space=pl.ANY)
-    tables = azimuth_tables()
-    image, terms = pl.pallas_call(
-        functools.partial(azimuth_kernel, split=split),
-        out_shape=(
-            jax.ShapeDtypeStruct((2, 16, 16, 32, R2), BF16),
-            jax.ShapeDtypeStruct((LISTED, 512), BF16),
-        ),
-        in_specs=[hbm] * 7 + [vmem] * 3,
-        out_specs=(hbm, vmem),
-        scratch_shapes=[
-            pltpu.VMEM((4, 16, 16, 16, R2), BF16),
-            pltpu.VMEM((4, 16, 16, 16, R2), BF16),
-            pltpu.VMEM((16, 16, 4, 16, R2), BF16),
-            pltpu.VMEM((16, 16, 4, 16, R2), BF16),
-            pltpu.VMEM((16, 16, 2, 32, R2), F32),
-            *[pltpu.VMEM(t.shape, BF16) for t in tables],
-            pltpu.VMEM((2, 16, 16, 32, R2), BF16),
-            pltpu.VMEM((512, R2), F32),
-            pltpu.VMEM((R2, R2), BF16),
-            pltpu.VMEM((2, R2), jnp.int32),
-            pltpu.SemaphoreType.DMA((4, 3)),
-            pltpu.SemaphoreType.DMA((4,)),
-            pltpu.SemaphoreType.DMA,
-        ],
-        compiler_params=pltpu.CompilerParams(vmem_limit_bytes=62 * 2**20),
-        cost_estimate=pl.CostEstimate(flops=15 * 10**9, bytes_accessed=2 * 10**7, transcendentals=0),
-        name="azimuth_columns",
-    )(arrived, *[jnp.asarray(t) for t in tables], rate[None], listed, held)
-    return image.reshape(2, AZ, R2), terms
-
-
-def map_kernel(terms, blocks, out, got, rows, parts, sums, ends, sems):
-    form = lax.axis_index("form")
-    focus = lax.axis_index("focus")
-    row, ring = lax.rem(form, 8), lax.div(form, 8)
-
-    def wrapped(value, size):
-        return jnp.where(value >= size, value - size, value)
-
-    mates = [(form, wrapped(focus + d, 4)) for d in range(1, 4)]
-    across = [wrapped(row + d, 8) for d in range(1, 8)]
-    along = [wrapped(ring + d, 8) for d in range(1, 8)]
-    barrier = pltpu.get_barrier_semaphore()
-    for peer in mates + [(ring * 8 + r, focus) for r in across] + [(z * 8 + row, focus) for z in along]:
-        pl.semaphore_signal(barrier, inc=1, device_id=peer, device_id_type=MESH)
-    place = lax.broadcasted_iota(jnp.int32, (64, LISTED), 0)
-    own = (jnp.bitwise_and(place, 7) * 8 + jnp.right_shift(place, 3)) * 4 + focus
-    chosen = jnp.where(own == blocks[...], 1.0, 0.0).astype(BF16)
+    terms[...] = table[...].T[:LISTED].astype(BF16)
     pl.semaphore_wait(barrier, 17)
 
     def send(src, dst, i, peer):
@@ -598,26 +610,40 @@
         copy.wait_send()
 
 
-def own_map(terms, blocks):
+def own_map(image, listed, held, blocks):
     vmem = pl.BlockSpec(memory_space=pltpu.VMEM)
+    hbm = pl.BlockSpec(memory_space=pl.ANY)
+    tables = azimuth_tables()[:3]
     return pl.pallas_call(
-        map_kernel,
+        lines_kernel,
         out_shape=jax.ShapeDtypeStruct((1, 2 * R2), F32),
-        in_specs=[vmem, vmem],
+        in_specs=[hbm] * 4 + [vmem] * 3,
         out_specs=vmem,
         scratch_shapes=[
+            pltpu.VMEM((2, 16, 16, 32, R2), BF16),
+            pltpu.VMEM((4, 16, 16, 16, R2), BF16),
+            pltpu.VMEM((4, 16, 16, 16, R2), BF16),
+            pltpu.VMEM((16, 16, 4, 16, R2), BF16),
+            pltpu.VMEM((16, 16, 2, 32, R2), F32),
+            *[pltpu.VMEM(t.shape, BF16) for t in tables],
+            pltpu.VMEM((512, R2), F32),
+            pltpu.VMEM((R2, R2), BF16),
+            pltpu.VMEM((2, R2), jnp.int32),
+            pltpu.VMEM((LISTED, 512), BF16),
             pltpu.VMEM((3, LISTED, 512), BF16),
             pltpu.VMEM((64, 4, R2), F32),
             pltpu.VMEM((7, 8, 4, R2), F32),
             pltpu.VMEM((8, 4, R2), F32),
             pltpu.VMEM((7, 4, R2), F32),
+            pltpu.SemaphoreType.DMA((4,)),
+            pltpu.SemaphoreType.DMA((3,)),
             pltpu.SemaphoreType.DMA((34,)),
         ],
         compiler_params=pltpu.CompilerParams(
             has_side_effects=True, vmem_limit_bytes=62 * 2**20, collective_id=1
         ),
         name="phase_rows",
-    )(terms, blocks)
+    )(image, *[jnp.asarray(t) for t in tables], listed, held, blocks)
 
 
 def on_device(
@@ -631,8 +657,9 @@
     line_center,
 ):
     arrived = corner_turned(echoes, scale_rate, migration, range_phase)
-    focused_image, terms = focused(arrived, azimuth_rate, bright_columns, line_center)
-    phase_map = own_map(terms, line_block.reshape(1, LISTED))
+    image = focused(arrived, azimuth_rate)
+    phase_map = own_map(image, bright_columns, line_center, line_block.reshape(1, LISTED))
+    focused_image = image.reshape(2, AZ, R2)
     return (focused_image, phase_map)
 
 

time: 163 us -> 152 us (0.933)
  Pallas kernels: 161 us -> 150 us
    pallas_call x2, Pallas kernels: 45.4 us -> 35.6 us  [the longest x1 23 us: own_map(): pl.pallas_call(lines_kernel, out_shape=jax.ShapeDtypeStruct((1, 2 * R2),...]
where the time goes in v3:
time: 152 us
  Pallas kernels  150 us (99%)
    pallas_call x1, Pallas kernels, corner_turned(): pl.pallas_call(functools.partial(range_kernel, talk=talk), out_shape=jax....  115 us
    pallas_call x1, Pallas kernels, own_map(): pl.pallas_call(lines_kernel, out_shape=jax.ShapeDtypeStruct((1, 2 * R2),...  23 us
    pallas_call x1, Pallas kernels, focused(): pl.pallas_call(azimuth_kernel, out_shape=jax.ShapeDtypeStruct((2, 16, 16,...  12.6 us

profile of v3, /device:TPU:1, one launch (start us, length us, event | category | flops | bytes accessed | tf_op | source)
XLA Modules:
  0.0 152.0 jit_solution(6112700199300094129)
XLA Ops:
  0.6 114.5 %range_lines.1.z_hbm = bf16[16,16,4,16,128]{4,3,2,1,0:T(8,128)(2,1)} custom-call(bf16[2,32,32768]{2,1,0:T(8,128)(2,1)} %x_hbm.1, f32[32]{0:T(128)} %rate.1, f32[32]{0:T(128)} %shift.1, f32[256,128]{1,0:T(8,128)} %bitcast.6, bf16[512,512]{1,0:T(8,128)(2,1)} %constant.26.clone.args_0_, bf16[256,256]{1,0:T(8,128)(2,1)} %constant.27.clone.args_1_, ...), custom_call_target="tpu_custom_call" | custom-call | flops 7000000000 | bytes 10000000 | tf_op jit(solution)/shard_map/range_lines/pallas_call | solution.py:348
  115.2 12.6 %azimuth_columns.1.img_hbm = bf16[2,16,16,32,128]{4,3,2,1,0:T(8,128)(2,1)} custom-call(bf16[16,16,4,16,128]{4,3,2,1,0:T(8,128)(2,1)} %range_lines.1.z_hbm, bf16[16,256,256]{2,1,0:T(8,128)(2,1)} %constant.35.clone.t3, bf16[16,256,256]{2,1,0:T(8,128)(2,1)} %constant.36.clone.t4, bf16[4,256,256]{2,1,0:T(8,128)(2,1)} %constant.37.clone.t5, ...), custom_call_target="tpu_custom_call" | custom-call | flops 15000000512 | bytes 20000000 | tf_op jit(solution)/shard_map/azimuth_columns/pallas_call | solution.py:459
  127.8 23.0 %phase_rows.1 = f32[1,256]{1,0:T(1,128)} custom-call(bf16[2,16,16,32,128]{4,3,2,1,0:T(8,128)(2,1)} %azimuth_columns.1.img_hbm, bf16[16,256,256]{2,1,0:T(8,128)(2,1)} %constant.33.clone.args_7_.t1, bf16[4,256,256]{2,1,0:T(8,128)(2,1)} %constant.34.clone.args_8_.t2, bf16[16,256,256]{2,1,0:T(8,128)(2,1)} %constant.35.clone.t3, s32[1,32]{1,0:T(1,128)} %listed.1, ...), custom_call_target="tpu_custom_call" | custom-call | tf_op jit(solution)/shard_map/phase_rows/pallas_call | solution.py:617
  150.8 1.2 copy.27
